TPU v7x, 128 devices: a whole 4x4x4 slice. The times are simulated.
128 devices in a mesh: psg: 16 (over y, x), tp: 2 (over core), pb: 4 (over z).
Axes of the slice: x: 4, y: 4, z: 4, core: 2. Of those that a mesh axis runs over, the one named last changes fastest.
Arguments:
- tokens: bfloat16 [4, 32, 256, 4096], P('pb', 'psg', None, 'tp'), may hold values from -6 to 6
- lengths: int32 [4, 32], P('pb'), may hold values from 1 to 256, 5120 in all within a row
- enc_gain: float32 [4096], replicated, may hold values from 0.1 to 1.9
- w_query: bfloat16 [4096, 2048], P(None, 'tp'), may hold values from -1 to 1
- w_key: bfloat16 [4096, 2048], P(None, 'tp'), may hold values from -1 to 1
- w_value: bfloat16 [4096, 2048], P(None, 'tp'), may hold values from -0.09375 to 0.09375
- w_out: bfloat16 [2048, 4096], P('tp'), may hold values from -0.125 to 0.125
- final_gain: float32 [4096], replicated, may hold values from 0.1 to 1.9
- cross_key: bfloat16 [4096, 2048], P(None, 'tp'), may hold values from -1 to 1
- cross_value: bfloat16 [4096, 2048], P(None, 'tp'), may hold values from -0.09375 to 0.09375
- beam_states: bfloat16 [4, 4, 4096], P('pb'), may hold values from -6 to 6
- parents: int32 [4, 4], P('pb'), may hold values from 0 to 3
- dec_gain: float32 [4096], replicated, may hold values from 0.1 to 1.9
- dec_query: bfloat16 [4096, 2048], P('pb', 'tp'), may hold values from -1 to 1
Outputs:
- encoded: bfloat16 [4, 32, 256, 4096], P('pb', 'psg', None, 'tp')
- context: float32 [4, 4, 2048], P('pb', None, 'tp')
Inputs may be any that keep to these rules, and one draw needn't show every extreme that they name: The 32 lengths of each question sum to 5120; in each question some passage has length 256.
All inputs are finite; a program needn't handle non-finite values.
Results may differ from a plain program's by a relative error of at most 0.007.
Values may be sent and summed in bfloat16 or wider, within the bound.
A program may use at most 256 MiB of HBM per device.

v0:
```python
import jax
import jax.numpy as jnp
from jax import lax
from jax.sharding import PartitionSpec as P

DH = 64


EPS = 1e-06
SCALE = 0.125
NEGATIVE = -1e30


def rms_scale(entries, gain_vec, model_width):
    entries = entries.astype(jnp.float32)
    inverse = lax.rsqrt(jnp.sum(entries * entries, axis=-1, keepdims=True) / model_width + EPS)
    return entries * inverse * gain_vec


def attend_piece(running, queries, key_rows, value_rows, live_lengths):
    peak_old, total_old, weighted_old = running
    questions, count, passage_len, flat_cols = key_rows.shape
    heads_local = queries.shape[2]
    key_heads = key_rows.reshape(questions, count * passage_len, heads_local, DH)
    value_heads = value_rows.reshape(questions, count * passage_len, heads_local, DH)
    scores = (
        jnp.einsum("qbhd,qkhd->qbhk", queries, key_heads, preferred_element_type=jnp.float32)
        * SCALE
    )
    slot_index = lax.broadcasted_iota(jnp.int32, (questions, count, passage_len), 2)
    live_mask = (slot_index < live_lengths[:, :, None]).reshape(
        questions, 1, 1, count * passage_len
    )
    peak_new = jnp.maximum(peak_old, jnp.max(jnp.where(live_mask, scores, NEGATIVE), axis=-1))
    expo_terms = jnp.where(live_mask, jnp.exp(scores - peak_new[..., None]), 0.0)
    total_new = jnp.sum(expo_terms, axis=-1)
    weighted_new = jnp.einsum(
        "qbhk,qkhd->qbhd",
        expo_terms.astype(jnp.bfloat16),
        value_heads,
        preferred_element_type=jnp.float32,
    )
    return (peak_new, total_new, weighted_new)


def per_device(
    tokens,
    lengths,
    enc_gain,
    w_query,
    w_key,
    w_value,
    w_out,
    final_gain,
    cross_key,
    cross_value,
    beam_states,
    parents,
    dec_gain,
    dec_query,
):
    questions, passages, passage_len, local_cols = tokens.shape
    model_width = local_cols * lax.axis_size("tp")
    heads_local = w_query.shape[1] // DH
    beam_count = beam_states.shape[1]
    row_count = questions * passages * passage_len
    first_slot = lax.axis_index("psg") * passages
    local_lengths = lax.dynamic_slice_in_dim(lengths, first_slot, passages, 1)
    gathered = lax.all_gather(tokens, "tp", axis=3, tiled=True)
    gathered_rows = gathered.reshape(row_count, model_width)
    normed = rms_scale(gathered_rows, enc_gain, model_width).astype(jnp.bfloat16)

    def project(matrix):
        product = jnp.dot(normed, matrix, preferred_element_type=jnp.float32)
        return product.astype(jnp.bfloat16).reshape(
            questions * passages, passage_len, heads_local, DH
        )

    queries_enc = project(w_query)
    keys_enc = project(w_key)
    values_enc = project(w_value)
    scores = (
        jnp.einsum("nihd,njhd->nhij", queries_enc, keys_enc, preferred_element_type=jnp.float32)
        * SCALE
    )
    slot_index = lax.broadcasted_iota(jnp.int32, (questions * passages, passage_len), 1)
    key_mask = (slot_index < local_lengths.reshape(questions * passages, 1))[:, None, None, :]
    peak = jnp.max(jnp.where(key_mask, scores, NEGATIVE), axis=-1, keepdims=True)
    expo_terms = jnp.where(key_mask, jnp.exp(scores - peak), 0.0)
    denom = jnp.sum(expo_terms, axis=-1, keepdims=True)
    blended = jnp.einsum(
        "nhij,njhd->nihd",
        expo_terms.astype(jnp.bfloat16),
        values_enc,
        preferred_element_type=jnp.float32,
    )
    blended = blended / jnp.transpose(denom, (0, 2, 1, 3))
    attended = blended.astype(jnp.bfloat16).reshape(row_count, heads_local * DH)
    partial_value = jnp.dot(attended, w_out, preferred_element_type=jnp.float32)
    column_share = lax.psum_scatter(
        partial_value.astype(jnp.bfloat16), "tp", scatter_dimension=1, tiled=True
    ).astype(jnp.float32)
    encoded_local = (
        tokens.reshape(row_count, local_cols).astype(jnp.float32) + column_share
    ).astype(jnp.bfloat16)
    encoded_wide = encoded_local.astype(jnp.float32)
    squares = lax.psum(jnp.sum(encoded_wide * encoded_wide, axis=-1), "tp")
    inverse = lax.rsqrt(squares / model_width + EPS)
    gain_part = lax.dynamic_slice_in_dim(
        final_gain, lax.axis_index("tp") * local_cols, local_cols, 0
    )
    final_local = (encoded_wide * inverse[:, None] * gain_part).astype(jnp.bfloat16)
    block_part = lax.all_gather(final_local, "tp", axis=1, tiled=True)
    key_next = jnp.dot(block_part, cross_key, preferred_element_type=jnp.float32)
    value_next = jnp.dot(block_part, cross_value, preferred_element_type=jnp.float32)
    ckey = key_next.astype(jnp.bfloat16).reshape(questions, passages, passage_len, heads_local * DH)
    cval = value_next.astype(jnp.bfloat16).reshape(
        questions, passages, passage_len, heads_local * DH
    )
    beam_index = lax.broadcasted_iota(jnp.int32, (questions, beam_count, beam_count), 2)
    one_hot = (parents[:, :, None] == beam_index).astype(jnp.bfloat16)
    chosen = jnp.einsum("qbc,qcd->qbd", one_hot, beam_states, preferred_element_type=jnp.float32)
    dec_normed = rms_scale(chosen, dec_gain, model_width).astype(jnp.bfloat16)
    full_rows = lax.all_gather(dec_query, "pb", axis=0, tiled=True)
    dquery = jnp.einsum("qbd,dh->qbh", dec_normed, full_rows, preferred_element_type=jnp.float32)
    queries = dquery.astype(jnp.bfloat16).reshape(questions, beam_count, heads_local, DH)
    start_carry = (
        jnp.full((questions, beam_count, heads_local), NEGATIVE, jnp.float32),
        jnp.zeros((questions, beam_count, heads_local), jnp.float32),
        jnp.zeros((questions, beam_count, heads_local, DH), jnp.float32),
    )
    peak_all, total_all, weighted_all = attend_piece(
        start_carry,
        queries,
        lax.all_gather(ckey, "psg", axis=1, tiled=True),
        lax.all_gather(cval, "psg", axis=1, tiled=True),
        lengths,
    )
    context = (weighted_all / total_all[..., None]).reshape(questions, beam_count, heads_local * DH)
    return (encoded_local.reshape(questions, passages, passage_len, local_cols), context)


def solution(mesh):
    in_specs = (
        P("pb", "psg", None, "tp"),
        P("pb", None),
        P(),
        P(None, "tp"),
        P(None, "tp"),
        P(None, "tp"),
        P("tp", None),
        P(),
        P(None, "tp"),
        P(None, "tp"),
        P("pb", None, None),
        P("pb", None),
        P(),
        P("pb", "tp"),
    )
    out_specs = (P("pb", "psg", None, "tp"), P("pb", None, "tp"))
    return jax.shard_map(
        per_device, mesh=mesh, in_specs=in_specs, out_specs=out_specs, check_vma=False
    )
```

profile of v0, /device:TPU:0, one launch (start us, length us, event | category | flops | bytes accessed | tf_op | source)
XLA Modules:
  0.0 510.1 jit_solution(14024390260368349655)
XLA Ops:
  7.2 0.7 all-gather.6.cloned.1.call-update
  8.0 0.7 dynamic-slice_bitcast_fusion
  8.7 0.1 iota_compare_fusion.1
  8.8 19.7 %all-gather.6.cloned.1.call-done = bf16[1,2,256,4096]{3,2,1,0:T(8,128)(2,1)} async-done(((bf16[1,2,256,2048]{3,2,1,0:T(8,128)(2,1)}), bf16[1,2,256,4096]{3,2,1,0:T(8,128)(2,1)}) %all-gather.6.cloned.1.call-update) | async-done | bytes 4194320 | tf_op jit(solution)/shard_map/all_gather | solution.py:69
  28.5 3.2 multiply_reduce_fusion
  31.8 0.2 copy-done.2
  32.0 1.7 fusion.3
  33.6 2.1 copy-done.4
  35.8 1.1 copy-done.10
  36.9 4.6 convolution_convert_fusion.3
  41.5 1.8 reshape.228
  43.3 9.3 %convolution_convert_fusion.4 = bf16[512,1024]{1,0:T(8,128)(2,1)S(1)} fusion(bf16[512,4096]{1,0:T(8,128)(2,1)} %copy-done.4, bf16[4096,1024]{1,0:T(8,128)(2,1)} %param.17), kind=kOutput, calls=%fused_computation.35 | convolution fusion | flops 4295491584 | bytes 13631488 | tf_op jit(solution)/shard_map/dot_general | solution.py:74
  52.6 8.0 %convolution_convert_fusion.5 = bf16[512,1024]{1,0:T(8,128)(2,1)} fusion(bf16[512,4096]{1,0:T(8,128)(2,1)S(1)} %copy-done.5, bf16[4096,1024]{1,0:T(8,128)(2,1)} %param.19), kind=kOutput, calls=%fused_computation.36 | convolution fusion | flops 4295491584 | bytes 13631488 | tf_op jit(solution)/shard_map/dot_general | solution.py:74
  60.6 4.0 reshape.226
  64.6 2.3 reshape.227
  66.9 2.9 fusion.18
  69.7 4.0 fusion.46
  73.8 1.0 fusion.17
  74.8 1.1 copy.42
  75.9 0.2 copy.57
  76.1 9.5 %convolution_convert_fusion = bf16[512,4096]{1,0:T(8,128)(2,1)} fusion(bf16[512,1024]{0,1:T(8,128)(2,1)S(1)} %bitcast.95, bf16[1024,4096]{1,0:T(8,128)(2,1)} %param.20), kind=kOutput, calls=%fused_computation.11 | convolution fusion | flops 4297064448 | bytes 13631488 | tf_op jit(solution)/shard_map/dot_general | solution.py:99
  85.6 0.0 all-gather.8.cloned.1.call-start
  85.7 16.3 %reduce-scatter.2.cloned.1.call-done = bf16[512,2048]{1,0:T(8,128)(2,1)} async-done(((bf16[512,4096]{1,0:T(8,128)(2,1)}), bf16[512,2048]{1,0:T(8,128)(2,1)}) %reduce-scatter.2.cloned.1.call-update) | async-done | bytes 2097168 | tf_op jit(solution)/shard_map/reduce_scatter | solution.py:100
  102.0 3.9 fusion.8
  105.9 2.4 psum.7
  108.3 3.5 fusion.10
  111.8 0.0 all-gather.14.cloned.1.call-start
  111.9 0.5 all-gather.14.cloned.1.call-update
  112.4 0.0 all-gather.12.cloned.1.call-start
  112.5 17.2 %all-gather.8.cloned.1.call-done = bf16[512,4096]{1,0:T(8,128)(2,1)} async-done(((bf16[512,2048]{1,0:T(8,128)(2,1)}), bf16[512,4096]{1,0:T(8,128)(2,1)}) %all-gather.8.cloned.1.call-update) | async-done | bytes 4194320 | tf_op jit(solution)/shard_map/all_gather | solution.py:113
  129.7 10.1 %convolution_convert_fusion.1 = bf16[512,1024]{1,0:T(8,128)(2,1)} fusion(bf16[512,4096]{1,0:T(8,128)(2,1)} %all-gather.8.cloned.1.call-done, bf16[4096,1024]{1,0:T(8,128)(2,1)} %param.22), kind=kOutput, calls=%fused_computation.32 | convolution fusion | flops 4295491584 | bytes 13631488 | tf_op jit(solution)/shard_map/dot_general | solution.py:114
  139.9 0.3 all-gather.10.cloned.1.call-start
  140.1 11.6 %convolution_convert_fusion.2 = bf16[512,1024]{1,0:T(8,128)(2,1)} fusion(bf16[512,4096]{1,0:T(8,128)(2,1)} %all-gather.8.cloned.1.call-done, bf16[4096,1024]{1,0:T(8,128)(2,1)} %param.23), kind=kOutput, calls=%fused_computation.33 | convolution fusion | flops 4295491584 | bytes 13631488 | tf_op jit(solution)/shard_map/dot_general | solution.py:115
  151.8 0.1 lt.41
  151.9 0.3 multiply_reduce_fusion.1
  152.3 63.8 %all-gather.14.cloned.1.call-done = bf16[4096,1024]{1,0:T(8,128)(2,1)} async-done(((bf16[1024,1024]{1,0:T(8,128)(2,1)}), bf16[4096,1024]{1,0:T(8,128)(2,1)}) %all-gather.14.cloned.1.call-update) | async-done | bytes 8388624 | tf_op jit(solution)/shard_map/all_gather | solution.py:124
  216.1 4.6 convolution_convert_fusion.6
  220.7 0.1 reshape.221
  220.8 109.5 %all-gather.12.cloned.1.call-done = bf16[1,32,256,1024]{3,2,0,1:T(8,128)(2,1)} async-done(((bf16[1,2,256,1024]{3,2,0,1:T(8,128)(2,1)}), bf16[1,32,256,1024]{3,2,0,1:T(8,128)(2,1)}) %all-gather.12.cloned.1.call-update) | async-done | bytes 16777232 | tf_op jit(solution)/shard_map/all_gather | solution.py:135
  330.3 24.2 %copy.46 = bf16[1,32,256,1024]{2,1,3,0:T(8,128)(2,1)} copy(bf16[1,32,256,1024]{3,2,0,1:T(8,128)(2,1)} %all-gather.12.cloned.1.call-done) | data formatting | bytes 33554432 | tf_op jit(solution)/shard_map/all_gather | solution.py:135
  354.5 25.9 %reshape.219 = bf16[8192,16,64]{0,2,1:T(8,128)(2,1)} reshape(bf16[1,32,256,1024]{2,1,3,0:T(8,128)(2,1)} %copy.46) | data formatting | bytes 33554432 | tf_op jit(solution)/shard_map/reshape.10
  380.4 7.4 %select_reduce_fusion.1 = (f32[4,16]{0,1:T(8,128)S(1)}, f32[1,4,16,8192]{3,1,2,0:T(4,128)S(1)}) fusion(pred[8192]{0:T(1024)(128)(4,1)S(1)} %lt.43, bf16[8192,16,64]{0,2,1:T(8,128)(2,1)} %reshape.219, bf16[4,16,64]{2,1,0:T(8,128)(2,1)S(1)} %reshape.221), kind=kOutput, calls=%fused_computation.31 | convolution fusion | flops 68681664 | bytes 18891008 | tf_op jit(solution)/shard_map/qbhd,qkhd->qbhk/dot_general | solution.py:27
  387.8 55.6 %all-gather.10.cloned.1.call-done = bf16[1,32,256,1024]{3,2,0,1:T(8,128)(2,1)} async-done(((bf16[1,2,256,1024]{3,2,0,1:T(8,128)(2,1)}), bf16[1,32,256,1024]{3,2,0,1:T(8,128)(2,1)}) %all-gather.10.cloned.1.call-update) | async-done | bytes 16777232 | tf_op jit(solution)/shard_map/all_gather | solution.py:136
  443.5 23.9 %copy.44 = bf16[1,32,256,1024]{2,1,3,0:T(8,128)(2,1)} copy(bf16[1,32,256,1024]{3,2,0,1:T(8,128)(2,1)} %all-gather.10.cloned.1.call-done) | data formatting | bytes 33554432 | tf_op jit(solution)/shard_map/all_gather | solution.py:136
  467.4 25.6 %reshape.217 = bf16[8192,16,64]{0,2,1:T(8,128)(2,1)} reshape(bf16[1,32,256,1024]{2,1,3,0:T(8,128)(2,1)} %copy.44) | data formatting | bytes 33554432 | tf_op jit(solution)/shard_map/reshape.30
  493.0 1.1 fusion.22
  494.2 8.1 %fusion.28 = f32[1,4,16,64]{3,1,2,0:T(4,128)S(1)} fusion(bf16[8192,16,64]{0,2,1:T(8,128)(2,1)} %reshape.217, f32[1,4,16,8192]{3,1,2,0:T(4,128)S(1)} %get-tuple-element.9, f32[4,16]{0,1:T(8,128)S(1)} %broadcast_maximum_fusion, pred[8192]{0:T(1024)(128)(4,1)S(1)} %lt.43, f32[4,16]{0,1:T(8,128)S(1)} %fusion.22), kind=kOutput, calls=%fused_computation.41 | convolution fusion | flops 68685824 | bytes 18899456 | tf_op jit(solution)/shard_map/qbhk,qkhd->qbhd/dot_general | solution.py:37
  502.3 0.7 reshape.223
  (38 shorter events, 0.3 us)
Async XLA Ops:
  7.2 144.8 %copy-start = (bf16[1,4,4096]{2,1,0:T(4,128)(2,1)S(1)}, bf16[1,4,4096]{2,1,0:T(4,128)(2,1)}, u32[]{:S(2)}) copy-start(bf16[1,4,4096]{2,1,0:T(4,128)(2,1)} %param.24) | copy-start | bytes 98308
  7.2 24.6 %copy-start.8 = (f32[4096]{0:T(1024)S(1)}, f32[4096]{0:T(1024)}, u32[]{:S(2)}) copy-start(f32[4096]{0:T(1024)} %param.16) | copy-start | bytes 49156
  7.2 21.3 %all-gather.6.cloned.1.call-start = ((), (), s32[]{:S(2)}) async-start(), calls=%async_computation.1 | async-start | bytes 6291456 | tf_op jit(solution)/shard_map/all_gather | solution.py:69
  7.9 94.1 %reduce-scatter.2.cloned.1.call-start = ((), (), s32[]{:S(2)}) async-start(), calls=%async_computation.2 | async-start | bytes 6291456 | tf_op jit(solution)/shard_map/reduce_scatter | solution.py:100
  28.5 3.4 copy-start.2
  32.0 4.9 copy-start.10
  33.6 2.1 copy-start.4
  43.3 9.3 %copy-start.5 = (bf16[512,4096]{1,0:T(8,128)(2,1)S(1)}, bf16[512,4096]{1,0:T(8,128)(2,1)}, u32[]{:S(2)}) copy-start(bf16[512,4096]{1,0:T(8,128)(2,1)} %copy-done.4) | copy-start | bytes 12582916
  69.7 4.0 copy-start.6
  85.6 16.4 %copy-start.3 = (bf16[1,2,256,2048]{3,2,1,0:T(8,128)(2,1)S(1)}, bf16[1,2,256,2048]{3,2,1,0:T(8,128)(2,1)}, u32[]{:S(2)}) copy-start(bf16[1,2,256,2048]{3,2,1,0:T(8,128)(2,1)} %param.14) | copy-start | bytes 6291460
  85.6 44.1 %all-gather.8.cloned.1.call-start = ((), (), s32[]{:S(2)}) async-start(), calls=%async_computation.3 | async-start | bytes 6291456 | tf_op jit(solution)/shard_map/all_gather | solution.py:113
  85.7 22.7 %dynamic-slice-start = ((f32[4096]{0:T(1024)}, s32[]{:T(128)}), f32[2048]{0:T(1024)S(1)}, s32[]{:S(2)}) async-start(f32[4096]{0:T(1024)} %param.21, s32[]{:T(128)} %select_n.23), calls=%async_computation.7 | async-start | bytes 16896 | tf_op jit(solution)/shard_map/dynamic_slice | solution.py:109
  111.8 104.2 %all-gather.14.cloned.1.call-start = ((), (), s32[]{:S(2)}) async-start(), calls=%async_computation.6 | async-start | bytes 10485760 | tf_op jit(solution)/shard_map/all_gather | solution.py:124
  112.4 217.9 %all-gather.12.cloned.1.call-start = ((), (), s32[]{:S(2)}) async-start(), calls=%async_computation.5 | async-start | bytes 17825792 | tf_op jit(solution)/shard_map/all_gather | solution.py:135
  139.8 12.0 %copy-start.9 = (s32[1,32]{1,0:T(1,128)S(1)}, s32[1,32]{1,0:T(1,128)}, u32[]{:S(2)}) copy-start(s32[1,32]{1,0:T(1,128)} %param.15) | copy-start | bytes 388
  139.8 12.1 %copy-start.11 = (s32[1,4]{1,0:T(1,128)S(1)}, s32[1,4]{1,0:T(1,128)}, u32[]{:S(2)}) copy-start(s32[1,4]{1,0:T(1,128)} %param.25) | copy-start | bytes 52
  139.9 76.2 %copy-start.7 = (f32[4096]{0:T(1024)S(1)}, f32[4096]{0:T(1024)}, u32[]{:S(2)}) copy-start(f32[4096]{0:T(1024)} %param.26) | copy-start | bytes 49156
  139.9 303.6 %all-gather.10.cloned.1.call-start = ((), (), s32[]{:S(2)}) async-start(), calls=%async_computation.4 | async-start | bytes 17825792 | tf_op jit(solution)/shard_map/all_gather | solution.py:136
  494.2 8.8 %copy-start.1 = (bf16[1,4,4096]{2,1,0:T(4,128)(2,1)S(1)}, bf16[1,4,4096]{2,1,0:T(4,128)(2,1)}, u32[]{:S(2)}) copy-start(bf16[1,4,4096]{2,1,0:T(4,128)(2,1)} %param.24) | copy-start | bytes 98308
Sparse Core Ops, SparseCore 0:
  9.7 18.7 all-gather.5
  85.8 16.2 reduce-scatter.1
  111.9 17.6 all-gather.7
  131.3 84.7 all-gather.13
  218.3 111.9 all-gather.11
  332.5 110.8 all-gather.9
where the time goes:
time: 518 us; the launch traced here: 510 us
  waiting for transfers between devices  283 us (55%)
  local copies, waits for them, and re-layouts  114 us (22%)
  matrix products  77.4 us (15%)
  other arithmetic  17.5 us (3%)
  between operations  14.6 us (3%)
    all_gather x1, waiting for transfers between devices, per_device(): lax.all_gather(ckey, 'psg', axis=1, tiled=True)  110 us
    all_gather x1, waiting for transfers between devices, per_device(): full_rows = lax.all_gather(dec_query, 'pb', axis=0, tiled=True)  63.8 us
    all_gather x1, waiting for transfers between devices, per_device(): lax.all_gather(cval, 'psg', axis=1, tiled=True)  55.6 us
    another operation x3, local copies, waits for them, and re-layouts  51.7 us
    all_gather x1, local copies, waits for them, and re-layouts, per_device(): lax.all_gather(ckey, 'psg', axis=1, tiled=True)  24.2 us
    all_gather x1, local copies, waits for them, and re-layouts, per_device(): lax.all_gather(cval, 'psg', axis=1, tiled=True)  23.9 us
    dot_general x3, matrix products, project(): product = jnp.dot(normed, matrix, preferred_element_type=jnp.float32)  21.9 us
    all_gather x1, waiting for transfers between devices, per_device(): gathered = lax.all_gather(tokens, 'tp', axis=3, tiled=True)  19.7 us
  transfers between devices with their start and end apart: 6, of which 6 were waited for; matrix products, arithmetic and copies ran while one was open for 17% of the time, Pallas kernels for 0%

commit v1 on v0

v1 whole, which is shorter than its diff:
```python
import jax
import jax.numpy as jnp
from jax import lax
from jax.sharding import PartitionSpec as P

DH = 64


EPS = 1e-06
SCALE = 0.125
NEGATIVE = -1e30


def rms_scale(entries, gain_vec, model_width):
    entries = entries.astype(jnp.float32)
    inverse = lax.rsqrt(jnp.sum(entries * entries, axis=-1, keepdims=True) / model_width + EPS)
    return entries * inverse * gain_vec


def per_device(
    tokens,
    lengths,
    enc_gain,
    w_query,
    w_key,
    w_value,
    w_out,
    final_gain,
    cross_key,
    cross_value,
    beam_states,
    parents,
    dec_gain,
    dec_query,
):
    questions, passages, passage_len, local_cols = tokens.shape
    tp = lax.axis_size("tp")
    pb = lax.axis_size("pb")
    model_width = local_cols * tp
    heads = w_query.shape[1] // DH
    beams = beam_states.shape[1]
    rows = questions * passages * passage_len
    first_slot = lax.axis_index("psg") * passages
    local_lengths = lax.dynamic_slice_in_dim(lengths, first_slot, passages, 1)

    all_states = lax.all_gather(beam_states, "pb", axis=0, tiled=True)
    all_parents = lax.all_gather(parents, "pb", axis=0, tiled=True)
    beam_index = lax.broadcasted_iota(jnp.int32, (pb, beams, beams), 2)
    one_hot = (all_parents[:, :, None] == beam_index).astype(jnp.bfloat16)
    chosen = jnp.einsum("qbc,qcd->qbd", one_hot, all_states, preferred_element_type=jnp.float32)
    dec_normed = rms_scale(chosen, dec_gain, model_width).astype(jnp.bfloat16)
    depth = dec_query.shape[0]
    dec_part = lax.dynamic_slice_in_dim(dec_normed, lax.axis_index("pb") * depth, depth, 2)
    dq_part = jnp.dot(dec_part.reshape(pb * beams, depth), dec_query, preferred_element_type=jnp.float32)
    dquery = lax.psum_scatter(dq_part, "pb", scatter_dimension=0, tiled=True)
    dquery = dquery.astype(jnp.bfloat16).reshape(beams, heads, DH)
    absorbed = jnp.einsum(
        "mhd,bhd->mhb", cross_key.reshape(model_width, heads, DH), dquery, preferred_element_type=jnp.float32
    ).reshape(model_width, heads * beams)
    absorbed = lax.all_to_all(absorbed.astype(jnp.bfloat16), "tp", 0, 1, tiled=True)

    gathered_rows = lax.all_gather(tokens, "tp", axis=3, tiled=True).reshape(rows, model_width)
    normed = rms_scale(gathered_rows, enc_gain, model_width).astype(jnp.bfloat16)

    def project(matrix):
        product = jnp.dot(normed, matrix, preferred_element_type=jnp.float32)
        return product.astype(jnp.bfloat16).reshape(passages, passage_len, heads, DH)

    queries_enc = project(w_query)
    keys_enc = project(w_key)
    values_enc = project(w_value)
    scores = (
        jnp.einsum("nihd,njhd->nhij", queries_enc, keys_enc, preferred_element_type=jnp.float32)
        * SCALE
    )
    slot_index = lax.broadcasted_iota(jnp.int32, (passages, passage_len), 1)
    live = slot_index < local_lengths.reshape(passages, 1)
    key_mask = live[:, None, None, :]
    peak = jnp.max(jnp.where(key_mask, scores, NEGATIVE), axis=-1, keepdims=True)
    expo_terms = jnp.where(key_mask, jnp.exp(scores - peak), 0.0)
    denom = jnp.sum(expo_terms, axis=-1, keepdims=True)
    blended = jnp.einsum(
        "nhij,njhd->nihd",
        expo_terms.astype(jnp.bfloat16),
        values_enc,
        preferred_element_type=jnp.float32,
    )
    blended = blended / jnp.transpose(denom, (0, 2, 1, 3))
    attended = blended.astype(jnp.bfloat16).reshape(rows, heads * DH)
    partial_value = jnp.dot(attended, w_out, preferred_element_type=jnp.float32)
    column_share = lax.psum_scatter(
        partial_value.astype(jnp.bfloat16), "tp", scatter_dimension=1, tiled=True
    ).astype(jnp.float32)
    encoded_local = (
        tokens.reshape(rows, local_cols).astype(jnp.float32) + column_share
    ).astype(jnp.bfloat16)
    encoded_wide = encoded_local.astype(jnp.float32)
    squares = lax.psum(jnp.sum(encoded_wide * encoded_wide, axis=-1), "tp")
    inverse = lax.rsqrt(squares / model_width + EPS)
    gain_part = lax.dynamic_slice_in_dim(
        final_gain, lax.axis_index("tp") * local_cols, local_cols, 0
    )
    final_local = (encoded_wide * inverse[:, None] * gain_part).astype(jnp.bfloat16)
    part_scores = jnp.dot(final_local, absorbed, preferred_element_type=jnp.float32)
    cscores = lax.psum(part_scores, "tp") * SCALE
    live_rows = live.reshape(rows, 1)
    local_peak = jnp.max(jnp.where(live_rows, cscores, NEGATIVE), axis=0)
    cexp = jnp.where(live_rows, jnp.exp(cscores - local_peak), 0.0)
    total = jnp.sum(cexp, axis=0)
    mixed = lax.dot_general(
        cexp.astype(jnp.bfloat16), final_local, (((0,), (0,)), ((), ())), preferred_element_type=jnp.float32
    )
    mixed = lax.all_to_all(mixed.astype(jnp.bfloat16), "tp", 0, 1, tiled=True)
    part = jnp.einsum(
        "hbm,mhd->bhd",
        mixed.reshape(heads, beams, model_width),
        cross_value.reshape(model_width, heads, DH),
        preferred_element_type=jnp.float32,
    )
    mine = lax.axis_index("tp") * heads * beams
    my_peak = lax.dynamic_slice_in_dim(local_peak, mine, heads * beams, 0).reshape(heads, beams).T
    my_total = lax.dynamic_slice_in_dim(total, mine, heads * beams, 0).reshape(heads, beams).T
    whole_peak = lax.pmax(my_peak, "psg")
    factor = jnp.exp(my_peak - whole_peak)
    joined = jnp.concatenate([part * factor[..., None], (my_total * factor)[..., None]], axis=-1)
    joined = lax.psum(joined, "psg")
    context = joined[..., :DH] / joined[..., DH:]
    return (
        encoded_local.reshape(questions, passages, passage_len, local_cols),
        context.reshape(questions, beams, heads * DH),
    )


def solution(mesh):
    in_specs = (
        P("pb", "psg", None, "tp"),
        P("pb", None),
        P(),
        P(None, "tp"),
        P(None, "tp"),
        P(None, "tp"),
        P("tp", None),
        P(),
        P(None, "tp"),
        P(None, "tp"),
        P("pb", None, None),
        P("pb", None),
        P(),
        P("pb", "tp"),
    )
    out_specs = (P("pb", "psg", None, "tp"), P("pb", None, "tp"))
    return jax.shard_map(
        per_device, mesh=mesh, in_specs=in_specs, out_specs=out_specs, check_vma=False
    )
```

time: 518 us -> 318 us (0.61); the launches traced: 510 us -> 317 us
  waiting for transfers between devices: 283 us -> 33.2 us
  blocking collectives: 2.44 us -> 154 us
  local copies, waits for them, and re-layouts: 114 us -> 42.8 us
  matrix products: 77.4 us -> 52.4 us
    all_gather x5 -> x1, waiting for transfers between devices: 266 us -> 19.7 us  [per_device(): lax.all_gather(tokens, 'tp', axis=3, tiled=True).reshape(rows, model_width)]
    psum x0 -> x1, blocking collectives: none -> 69.5 us  [per_device(): joined = lax.psum(joined, 'psg')]
    another operation x3 -> x0, local copies, waits for them, and re-layouts: 51.7 us -> none
    all_gather x2 -> x0, local copies, waits for them, and re-layouts: 48.1 us -> none  [the longest x1 24.2 us: per_device(): lax.all_gather(ckey, 'psg', axis=1, tiled=True)]
    pmax x0 -> x1, blocking collectives: none -> 41 us  [per_device(): whole_peak = lax.pmax(my_peak, 'psg')]
    dot_general x6, matrix products: 42.2 us -> 16.6 us  [the longest x1 5.64 us: per_device(): jnp.einsum('hbm,mhd->bhd', mixed.reshape(heads, beams, model_width), cros...]
    unnamed x28 -> x27, local copies, waits for them, and re-layouts: 3.73 us -> 27.4 us
    all_gather x0 -> x2, blocking collectives: none -> 21.9 us  [the longest x1 12 us: per_device(): all_states = lax.all_gather(beam_states, 'pb', axis=0, tiled=True)]
  transfers between devices with their start and end apart: 6 -> 4, of which waited for: 6 -> 2; matrix products, arithmetic and copies ran while one was open for 17% -> 11% of each run, Pallas kernels for 0% -> 0%
where the time goes in v1:
time: 318 us; the launch traced here: 317 us
  blocking collectives  154 us (48%)
  matrix products  52.4 us (16%)
  local copies, waits for them, and re-layouts  42.8 us (13%)
  waiting for transfers between devices  33.2 us (10%)
  other arithmetic  16 us (5%)
  between operations  14.7 us (5%)
  starting transfers between devices  3.6 us (1%)
    psum x1, blocking collectives, per_device(): joined = lax.psum(joined, 'psg')  69.5 us
    pmax x1, blocking collectives, per_device(): whole_peak = lax.pmax(my_peak, 'psg')  41 us
    unnamed x27, local copies, waits for them, and re-layouts  27.4 us
    dot_general x3, matrix products, project(): product = jnp.dot(normed, matrix, preferred_element_type=jnp.float32)  21.9 us
    all_gather x1, waiting for transfers between devices, per_device(): lax.all_gather(tokens, 'tp', axis=3, tiled=True).reshape(rows, model_width)  19.7 us
    unnamed x1, blocking collectives  14.8 us
    psum x1, waiting for transfers between devices, per_device(): cscores = lax.psum(part_scores, 'tp') * SCALE  12.8 us
    all_gather x1, blocking collectives, per_device(): all_states = lax.all_gather(beam_states, 'pb', axis=0, tiled=True)  12 us
  transfers between devices with their start and end apart: 4, of which 2 were waited for; matrix products, arithmetic and copies ran while one was open for 11% of the time, Pallas kernels for 0%

profile of v1, /device:TPU:0, one launch (start us, length us, event | category | flops | bytes accessed | tf_op | source)
XLA Modules:
  0.0 316.7 jit_solution(17189908860921823023)
XLA Ops:
  7.2 0.7 all-gather.3.cloned.1.call-update
  8.0 0.7 dynamic-slice_bitcast_fusion
  8.8 19.7 %all-gather.3.cloned.1.call-done = bf16[1,2,256,4096]{3,2,1,0:T(8,128)(2,1)} async-done(((bf16[1,2,256,2048]{3,2,1,0:T(8,128)(2,1)}), bf16[1,2,256,4096]{3,2,1,0:T(8,128)(2,1)}) %all-gather.3.cloned.1.call-update) | async-done | bytes 4194320 | tf_op jit(solution)/shard_map/all_gather | solution.py:62
  28.5 3.2 %multiply_reduce_fusion = f32[2,256]{1,0:T(2,128)S(1)} fusion(bf16[1,2,256,4096]{3,2,1,0:T(8,128)(2,1)} %all-gather.3.cloned.1.call-done), kind=kLoop, calls=%fused_computation.7 | loop fusion | flops 6290944 | bytes 4196352 | tf_op jit(solution)/shard_map/reduce_sum | solution.py:16
  32.0 1.7 fusion.2
  33.6 2.1 copy-done.2
  35.8 1.1 copy-done.9
  36.9 4.6 %convolution_convert_fusion.3 = bf16[512,1024]{1,0:T(8,128)(2,1)S(1)} fusion(bf16[512,4096]{1,0:T(8,128)(2,1)S(1)} %fusion.2, bf16[4096,1024]{1,0:T(8,128)(2,1)S(1)} %copy-done.9), kind=kOutput, calls=%fused_computation.31 | convolution fusion | flops 4295491584 | bytes 13631488 | tf_op jit(solution)/shard_map/dot_general | solution.py:66
  41.5 2.5 reshape.145
  44.0 9.3 %convolution_convert_fusion.4 = bf16[512,1024]{1,0:T(8,128)(2,1)S(1)} fusion(bf16[512,4096]{1,0:T(8,128)(2,1)} %copy-done.2, bf16[4096,1024]{1,0:T(8,128)(2,1)} %param.17), kind=kOutput, calls=%fused_computation.32 | convolution fusion | flops 4295491584 | bytes 13631488 | tf_op jit(solution)/shard_map/dot_general | solution.py:66
  53.3 8.0 %convolution_convert_fusion.5 = bf16[512,1024]{1,0:T(8,128)(2,1)} fusion(bf16[512,4096]{1,0:T(8,128)(2,1)S(1)} %copy-done.3, bf16[4096,1024]{1,0:T(8,128)(2,1)} %param.19), kind=kOutput, calls=%fused_computation.33 | convolution fusion | flops 4295491584 | bytes 13631488 | tf_op jit(solution)/shard_map/dot_general | solution.py:66
  61.3 4.1 %reshape.143 = bf16[2,256,16,64]{3,2,1,0:T(8,128)(2,1)} reshape(bf16[512,1024]{1,0:T(8,128)(2,1)} %convolution_convert_fusion.5) | data formatting | bytes 2097152 | tf_op jit(solution)/shard_map/reshape | solution.py:67
  65.3 2.3 reshape.144
  67.6 3.5 %fusion.18 = f32[2,16,256,256]{2,3,1,0:T(8,128)S(1)} fusion(bf16[2,256,16,64]{3,2,1,0:T(8,128)(2,1)} %reshape.145, bf16[2,256,16,64]{3,2,1,0:T(8,128)(2,1)} %reshape.144), kind=kOutput, calls=%fused_computation.27 | convolution fusion | flops 268435456 | bytes 10485760 | tf_op jit(solution)/shard_map/nihd,njhd->nhij/dot_general | solution.py:73
  71.1 4.0 %fusion.48 = (f32[2,16,256]{2,1,0:T(8,128)S(1)}, bf16[2,16,256,256]{2,3,1,0:T(8,128)(2,1)S(1)}) fusion(f32[2,16,256,256]{2,3,1,0:T(8,128)S(1)} %fusion.18, pred[2,256]{1,0:T(4,128)(4,1)S(1)} %iota_compare_fusion.2), kind=kOutput, calls=%fused_computation.68 | output fusion | flops 14680319 | bytes 12616192 | tf_op jit(solution)/shard_map/sub | solution.py:80
  75.2 1.0 fusion.17
  76.2 1.1 copy.53
  77.3 0.2 copy.74
  77.5 9.5 %convolution_convert_fusion = bf16[512,4096]{1,0:T(8,128)(2,1)} fusion(bf16[512,1024]{0,1:T(8,128)(2,1)S(1)} %bitcast.79, bf16[1024,4096]{1,0:T(8,128)(2,1)} %param.20), kind=kOutput, calls=%fused_computation.9 | convolution fusion | flops 4297064448 | bytes 13631488 | tf_op jit(solution)/shard_map/dot_general | solution.py:90
  87.0 0.6 copy-done.8
  87.7 9.9 %all-gather = s32[4,1,4]{2,1,0:T(1,128)S(1)} all-gather(s32[1,1,4]{2,1,0:T(1,128)S(1)} %bitcast.86), channel_id=1, replica_groups=mesh['psg'=16,'tp'=2,'pb'=4] {'pb'}, dimensions={0}, use_global_device_ids=true | all-gather | bytes 80 | tf_op jit(solution)/shard_map/all_gather | solution.py:47
  97.6 0.7 dynamic-slice.2
  98.3 12.0 %all_gather.11 = bf16[4,4,4096]{2,1,0:T(4,128)(2,1)S(1)} all-gather(bf16[1,4,4096]{2,1,0:T(4,128)(2,1)S(1)} %copy-done.5), channel_id=1, replica_groups=mesh['psg'=16,'tp'=2,'pb'=4] {'pb'}, dimensions={0}, use_global_device_ids=true | all-gather | bytes 163840 | tf_op jit(solution)/shard_map/all_gather | solution.py:46
  110.3 0.4 multiply_reduce_fusion.1
  110.8 0.6 dynamic-slice
  112.1 0.4 fusion.49
  112.4 14.8 %all-reduce = bf16[16,1024]{1,0:T(8,128)(2,1)S(1)} all-reduce(f32[16,1024]{1,0:T(8,128)S(1)} %fusion.49), channel_id=3, replica_groups=mesh['psg'=16,'tp'=2,'pb'=4] {'pb'}, use_global_device_ids=true, to_apply=%region_7.8.clone | all-reduce | flops 16384 | bytes 98304
  127.4 11.3 %copy.54 = bf16[4096,1024]{0,1:T(8,128)(2,1)} copy(bf16[4096,1024]{1,0:T(8,128)(2,1)} %param.22) | data formatting | bytes 16777216 | tf_op args[8]
  138.6 4.6 %fusion.7 = bf16[4096,16,4]{0,2,1:T(4,128)(2,1)S(1)} fusion(bf16[4096,16,64]{0,2,1:T(8,128)(2,1)} %bitcast.74, bf16[4,16,64]{2,1,0:T(8,128)(2,1)S(1)} %reshape.132), kind=kOutput, calls=%fused_computation.13 | convolution fusion | flops 33816576 | bytes 8921088 | tf_op jit(solution)/shard_map/mhd,bhd->mhb/dot_general | solution.py:57
  143.2 0.5 convert_element_type.91
  143.8 0.9 copy.56
  144.7 3.5 %all-to-all-start = ((bf16[2,2048,64]{1,2,0:T(8,128)(2,1)}), bf16[2,2048,64]{1,2,0:T(8,128)(2,1)S(1)}, u32[]{:S(2)}, u32[]{:S(2)}) async-start(bf16[2,2048,64]{1,2,0:T(8,128)(2,1)} %copy.56), calls=%async_computation.1 | async-start | bytes 1048576 | tf_op jit(solution)/shard_map/all_to_all | solution.py:60
  148.3 4.5 %fusion.8 = (f32[512]{0:T(512)S(1)}, bf16[512,2048]{1,0:T(8,128)(2,1)}) fusion(bf16[512,2048]{1,0:T(8,128)(2,1)} %reduce-scatter.2.cloned.1.call-done, bf16[1,2,256,2048]{3,2,1,0:T(8,128)(2,1)} %param.14), kind=kLoop, calls=%fused_computation.14 | loop fusion | flops 7339520 | bytes 6293504 | tf_op jit(solution)/shard_map/reduce_sum | solution.py:98
  152.8 2.5 psum.21
  155.4 3.1 fusion.28
  158.5 11.3 %copy.58 = bf16[4096,1024]{0,1:T(8,128)(2,1)} copy(bf16[4096,1024]{1,0:T(8,128)(2,1)} %param.23) | data formatting | bytes 16777216 | tf_op args[9]
  169.7 12.8 %all-reduce.3.cloned.1.call-done = f32[512,128]{1,0:T(8,128)} async-done(((f32[512,128]{1,0:T(8,128)}), f32[512,128]{1,0:T(8,128)}) %all-reduce.3.cloned.1.call-update) | async-done | bytes 262160 | tf_op jit(solution)/shard_map/psum | solution.py:105
  182.5 1.1 select_reduce_fusion.1
  183.7 1.1 fusion.30
  185.0 41.0 %pmax.7 = f32[4,16]{0,1:T(8,128)S(1)} all-reduce(f32[4,16]{0,1:T(8,128)S(1)} %bitcast.82), channel_id=1, replica_groups=mesh['psg'=16,'tp'=2,'pb'=4] {'psg'}, use_global_device_ids=true, to_apply=%region_10.11 | all-reduce | flops 64 | bytes 512 | tf_op jit(solution)/shard_map/pmax | solution.py:123
  226.0 0.2 copy.60
  226.2 2.6 convolution_convert_fusion.2
  228.8 4.2 %all_to_all.32 = bf16[2,64,2048]{2,1,0:T(8,128)(2,1)S(1)} all-to-all(bf16[2,64,2048]{2,1,0:T(8,128)(2,1)S(1)} %bitcast.81), channel_id=1, replica_groups=mesh['psg'=16,'tp'=2,'pb'=4] {'tp'}, dimensions={0} | all-to-all | bytes 1048576 | tf_op jit(solution)/shard_map/all_to_all | solution.py:113
  232.9 0.5 copy.57
  233.5 0.3 reshape.134
  233.8 5.6 %fusion.26 = f32[4,16,64]{2,0,1:T(4,128)S(1)} fusion(bf16[16,4,4096]{2,1,0:T(4,128)(2,1)S(1)} %reshape.134, bf16[4096,16,64]{0,2,1:T(8,128)(2,1)} %bitcast.75, f32[4,16]{0,1:T(8,128)S(1)} %get-tuple-element.3), kind=kOutput, calls=%fused_computation.35 | convolution fusion | flops 33558528 | bytes 8929536 | tf_op jit(solution)/shard_map/hbm,mhd->bhd/dot_general | solution.py:114
  239.5 69.5 %psum.23 = f32[4,16,65]{2,0,1:T(4,128)S(1)} all-reduce(f32[4,16,65]{2,0,1:T(4,128)S(1)} %pad_maximum_fusion), channel_id=1, replica_groups=mesh['psg'=16,'tp'=2,'pb'=4] {'psg'}, use_global_device_ids=true, to_apply=%region_12.13 | all-reduce | flops 4160 | bytes 33280 | tf_op jit(solution)/shard_map/psum | solution.py:126
  309.5 0.7 reshape.138
  (48 shorter events, 1.5 us)
Async XLA Ops:
  7.2 104.9 %copy-start = (bf16[1024,1024]{1,0:T(8,128)(2,1)S(1)}, bf16[1024,1024]{1,0:T(8,128)(2,1)}, u32[]{:S(2)}) copy-start(bf16[1024,1024]{1,0:T(8,128)(2,1)} %param.27) | copy-start | bytes 6291460
  7.2 24.6 %copy-start.6 = (f32[4096]{0:T(1024)S(1)}, f32[4096]{0:T(1024)}, u32[]{:S(2)}) copy-start(f32[4096]{0:T(1024)} %param.16) | copy-start | bytes 49156
  7.2 21.3 %all-gather.3.cloned.1.call-start = ((), (), s32[]{:S(2)}) async-start(), calls=%async_computation.3 | async-start | bytes 6291456 | tf_op jit(solution)/shard_map/all_gather | solution.py:62
  7.9 140.4 %reduce-scatter.2.cloned.1.call-start = ((), (), s32[]{:S(2)}) async-start(), calls=%async_computation.4 | async-start | bytes 6291456 | tf_op jit(solution)/shard_map/reduce_scatter | solution.py:91
  28.5 3.4 %copy-start.1 = (bf16[1,2,256,4096]{3,2,1,0:T(8,128)(2,1)S(1)}, bf16[1,2,256,4096]{3,2,1,0:T(8,128)(2,1)}, u32[]{:S(2)}) copy-start(bf16[1,2,256,4096]{3,2,1,0:T(8,128)(2,1)} %all-gather.3.cloned.1.call-done) | copy-start | bytes 12582916
  32.0 4.9 %copy-start.9 = (bf16[4096,1024]{1,0:T(8,128)(2,1)S(1)}, bf16[4096,1024]{1,0:T(8,128)(2,1)}, u32[]{:S(2)}) copy-start(bf16[4096,1024]{1,0:T(8,128)(2,1)} %param.18) | copy-start | bytes 25165828
  33.6 2.1 copy-start.2
  44.0 9.3 %copy-start.3 = (bf16[512,4096]{1,0:T(8,128)(2,1)S(1)}, bf16[512,4096]{1,0:T(8,128)(2,1)}, u32[]{:S(2)}) copy-start(bf16[512,4096]{1,0:T(8,128)(2,1)} %copy-done.2) | copy-start | bytes 12582916
  71.1 4.1 %copy-start.4 = (bf16[2,256,16,64]{3,2,1,0:T(8,128)(2,1)S(1)}, bf16[2,256,16,64]{3,2,1,0:T(8,128)(2,1)}, u32[]{:S(2)}) copy-start(bf16[2,256,16,64]{3,2,1,0:T(8,128)(2,1)} %reshape.143) | copy-start | bytes 3145732
  87.0 0.7 copy-start.8
  87.0 11.3 %copy-start.5 = (bf16[1,4,4096]{2,1,0:T(4,128)(2,1)S(1)}, bf16[1,4,4096]{2,1,0:T(4,128)(2,1)}, u32[]{:S(2)}) copy-start(bf16[1,4,4096]{2,1,0:T(4,128)(2,1)} %param.24) | copy-start | bytes 98308
  87.0 23.8 %copy-start.10 = (u32[128]{0:T(128)S(1)}, u32[128]{0:T(128)}, u32[]{:S(2)}) copy-start(u32[128]{0:T(128)} %constant.58) | copy-start | bytes 1540
  138.6 9.6 %copy-start.7 = (f32[4096]{0:T(1024)S(1)}, f32[4096]{0:T(1024)}, u32[]{:S(2)}) copy-start(f32[4096]{0:T(1024)} %param.21) | copy-start | bytes 49156
  144.7 10.7 %all-to-all-start = ((bf16[2,2048,64]{1,2,0:T(8,128)(2,1)}), bf16[2,2048,64]{1,2,0:T(8,128)(2,1)S(1)}, u32[]{:S(2)}, u32[]{:S(2)}) async-start(bf16[2,2048,64]{1,2,0:T(8,128)(2,1)} %copy.56), calls=%async_computation.1 | async-start | bytes 1048576 | tf_op jit(solution)/shard_map/all_to_all | solution.py:60
  148.2 34.3 %all-reduce.3.cloned.1.call-start = ((), (), s32[]{:S(2)}) async-start(), calls=%async_computation.5 | async-start | bytes 524288 | tf_op jit(solution)/shard_map/psum | solution.py:105
Sparse Core Ops, SparseCore 0:
  9.7 18.7 all-gather.2
  87.2 16.2 reduce-scatter.1
  158.6 23.8 all-reduce.2

commit v2 on v1

v2 whole, which is shorter than its diff:
```python
import functools

import jax
import jax.numpy as jnp
from jax import lax
from jax.experimental import pallas as pl
from jax.experimental.pallas import tpu as pltpu
from jax.sharding import PartitionSpec as P

DH = 64
EPS = 1e-06
SCALE = 0.125
LOG2E = 1.4426950408889634
NEGATIVE = -1e30
MESH = pl.DeviceIdType.MESH
F32 = jnp.float32
BF16 = jnp.bfloat16


def nt_dot(a, b):
    return lax.dot_general(a, b, (((1,), (1,)), ((), ())), preferred_element_type=F32)


def nn_dot(a, b):
    return jnp.dot(a, b, preferred_element_type=F32)


def lane_fold(x):
    total = x[:, :128]
    for i in range(1, x.shape[1] // 128):
        total = total + x[:, i * 128 : (i + 1) * 128]
    return total


def body(
    sizes,
    tok_hbm, len_ref, eg_ref, wq_hbm, wk_hbm, wv_hbm, wo_hbm, fg_ref, ck_hbm, cv_hbm, beam_ref, par_ref, dg_ref, dec_hbm,
    enc_hbm, ctx_ref,
    tok, xl, xr, wbuf, wo, acc, qkv, att, attp, enc, decw,
    sq, sqp, inv, gq, sc, scp, mix, mixp, bd, dn, dnr, dqp, dqr, stat, stats, ctp, cts,
    lsem, tsend, trecv, psend, precv, ssend, srecv, csend, crecv,
):
    npsg, npb = sizes
    rows, half = tok.shape
    width = 2 * half
    cols = qkv.shape[2]
    heads = cols // DH
    beams = beam_ref.shape[0]
    hb = heads * beams
    plen = 256
    passages = rows // plen
    tp = lax.axis_index("tp")
    psg = lax.axis_index("psg")
    pb = lax.axis_index("pb")
    other = 1 - tp
    mine_f = pl.ds(pl.multiple_of(tp * half, half), half)
    peer_f = pl.ds(pl.multiple_of(other * half, half), half)

    barrier = pltpu.get_barrier_semaphore()
    pl.semaphore_signal(barrier, inc=1, device_id={"tp": other}, device_id_type=MESH)

    def hello_psg(k, c):
        pl.semaphore_signal(barrier, inc=1, device_id={"psg": lax.rem(psg + k, npsg)}, device_id_type=MESH)
        return c

    lax.fori_loop(1, npsg, hello_psg, 0)
    for k in range(1, npb):
        pl.semaphore_signal(barrier, inc=1, device_id={"pb": lax.rem(pb + k, npb)}, device_id_type=MESH)

    copy_tok = pltpu.make_async_copy(tok_hbm, tok, lsem.at[0])
    copy_tok.start()
    w_hbm = (wq_hbm, wk_hbm, wv_hbm)
    copy_w = [[None, None] for _ in range(3)]
    for h, part in enumerate((mine_f, peer_f)):
        for w in range(3):
            copy_w[w][h] = pltpu.make_async_copy(w_hbm[w].at[part, :], wbuf.at[w, h], lsem.at[1 + 2 * w + h])
    copy_dec = pltpu.make_async_copy(dec_hbm, decw, lsem.at[7])
    copy_wo = pltpu.make_async_copy(wo_hbm.at[:, mine_f], wo.at[0], lsem.at[8])
    for w in range(3):
        copy_w[w][0].start()
    copy_dec.start()
    for w in range(3):
        copy_w[w][1].start()
    copy_wo.start()

    chosen = []
    for b in range(beams):
        row = jnp.zeros((1, width), F32)
        for c in range(beams):
            row = row + (par_ref[0, b] == c).astype(F32) * beam_ref[c : c + 1, :].astype(F32)
        chosen.append(row)
    depth = width // npb
    for b in range(beams):
        row = chosen[b]
        ms = jnp.sum(row * row, axis=-1, keepdims=True) * (1.0 / width) + EPS
        row = (row * lax.rsqrt(ms) * dg_ref[...]).astype(BF16).astype(F32)
        for j in range(npb):
            dn[j, b : b + 1, :] = row[:, j * depth : (j + 1) * depth]
    for j in range(npb):
        dn[j, beams:8, :] = jnp.zeros((8 - beams, depth), F32)

    blk = 32
    copy_tok.wait()

    def squares(i, c):
        r = pl.ds(pl.multiple_of(i * blk, blk), blk)
        x = tok[r, :].astype(F32)
        sq[r, :] = lane_fold(x * x)
        return c

    lax.fori_loop(0, rows // blk, squares, 0)

    pl.semaphore_wait(barrier, npsg - 1 + npb - 1 + 1)

    def to_other(src, dst, i):
        return pltpu.make_async_remote_copy(
            src_ref=src, dst_ref=dst, send_sem=tsend.at[i], recv_sem=trecv.at[i],
            device_id={"tp": other}, device_id_type=MESH,
        )

    send_sq = to_other(sq, sqp, 0)
    send_tok = to_other(tok, xr, 1)
    send_wo = to_other(wo_hbm.at[:, peer_f], wo.at[1], 2)
    send_sq.start()
    send_tok.start()

    def to_pb(k, src, dst, base):
        to = lax.rem(pb + k, npb)
        return pltpu.make_async_remote_copy(
            src_ref=src.at[to], dst_ref=dst.at[pb], send_sem=psend.at[base + k - 1], recv_sem=precv.at[base + k - 1],
            device_id={"pb": to}, device_id_type=MESH,
        )

    send_dn = [to_pb(k, dn, dnr, 0) for k in range(1, npb)]
    for s in send_dn:
        s.start()
    dnr[pb] = dn[pb]

    send_sq.wait()

    def normalise_local(i, c):
        r = pl.ds(pl.multiple_of(i * blk, blk), blk)
        ms = jnp.sum(sq[r, :] + sqp[r, :], axis=-1, keepdims=True) * (1.0 / width) + EPS
        v = jnp.broadcast_to(lax.rsqrt(ms), (blk, 128))
        inv[r, :] = v
        x = tok[r, :].astype(F32)
        xl[r, :] = (x * v[:, :1] * eg_ref[:, mine_f]).astype(BF16)
        return c

    lax.fori_loop(0, rows // blk, normalise_local, 0)

    nt = min(512, cols)
    for w in range(3):
        copy_w[w][0].wait()

        def first_half(j, c):
            t = pl.ds(pl.multiple_of(j * nt, nt), nt)
            acc[w, :, t] = nn_dot(xl[...], wbuf[w, 0, :, t])
            return c

        lax.fori_loop(0, cols // nt, first_half, 0)

    copy_ck = [
        pltpu.make_async_copy(ck_hbm.at[mine_f, :], wbuf.at[0, 0], lsem.at[9]),
        pltpu.make_async_copy(ck_hbm.at[peer_f, :], wbuf.at[1, 0], lsem.at[10]),
    ]
    copy_cv = [
        pltpu.make_async_copy(cv_hbm.at[mine_f, :], wbuf.at[2, 0], lsem.at[11]),
        pltpu.make_async_copy(cv_hbm.at[peer_f, :], wbuf.at[0, 1], lsem.at[12]),
    ]
    copy_ck[0].start()
    copy_ck[1].start()
    copy_cv[0].start()

    for s in send_dn:
        s.wait()
    copy_dec.wait()
    dqp[...] = nn_dot(dnr[...].reshape(npb * 8, depth).astype(BF16), decw[...]).reshape(npb, 8, cols)
    send_dq = [to_pb(k, dqp, dqr, npb - 1) for k in range(1, npb)]
    for s in send_dq:
        s.start()
    dqr[pb] = dqp[pb]

    send_tok.wait()
    send_wo.start()

    def normalise_peer(i, c):
        r = pl.ds(pl.multiple_of(i * blk, blk), blk)
        x = xr[r, :].astype(F32)
        xr[r, :] = (x * inv[r, :1] * eg_ref[:, peer_f]).astype(BF16)
        return c

    lax.fori_loop(0, rows // blk, normalise_peer, 0)

    for w in range(3):
        copy_w[w][1].wait()

        def second_half(j, c):
            t = pl.ds(pl.multiple_of(j * nt, nt), nt)
            qkv[w, :, t] = (acc[w, :, t] + nn_dot(xr[...], wbuf[w, 1, :, t])).astype(BF16)
            return c

        lax.fori_loop(0, cols // nt, second_half, 0)
        if w == 0:
            copy_cv[1].start()

    lane = lax.broadcasted_iota(jnp.int32, (plen, 128), 1)
    low = lane < DH
    slot = lax.broadcasted_iota(jnp.int32, (1, plen), 1)
    groups = cols // 256
    send_att = []
    for g in range(groups):
        for p in range(passages):
            key_live = slot < len_ref[0, psg * passages + p]
            r = slice(p * plen, (p + 1) * plen)
            for pair in range(2):
                t = slice(g * 256 + pair * 128, g * 256 + pair * 128 + 128)
                q = qkv[0, r, t]
                zero = jnp.zeros_like(q)
                q2 = jnp.concatenate([jnp.where(low, q, zero), jnp.where(low, zero, q)], axis=0)
                s = jnp.where(key_live, nt_dot(q2, qkv[1, r, t]), NEGATIVE)
                e = jnp.exp2((s - jnp.max(s, axis=-1, keepdims=True)) * (SCALE * LOG2E))
                den = jnp.sum(e, axis=-1, keepdims=True)
                o = nn_dot(e.astype(BF16), qkv[2, r, t]) / den
                att[r, t] = jnp.where(low, o[:plen], o[plen:]).astype(BF16)
        t = slice(g * 256, g * 256 + 256)
        s = to_other(att.at[:, t], attp.at[:, t], 3 + g)
        s.start()
        send_att.append(s)

    for s in send_dq:
        s.wait()
    dq = dqr[0]
    for j in range(1, npb):
        dq = dq + dqr[j]
    dq = dq.astype(BF16).astype(F32)
    head_of = lax.broadcasted_iota(jnp.int32, (heads, cols), 1) // DH
    head_row = lax.broadcasted_iota(jnp.int32, (heads, cols), 0)
    for b in range(beams):
        bd[b * heads : (b + 1) * heads, :] = jnp.where(head_of == head_row, dq[b : b + 1, :], 0.0).astype(BF16)
    mine_h = pl.ds(pl.multiple_of(tp * hb, hb), hb)
    peer_h = pl.ds(pl.multiple_of(other * hb, hb), hb)
    kt = min(512, half)

    for f in range(2):
        copy_ck[f].wait()

        def absorb(j, c):
            t = pl.ds(pl.multiple_of(j * kt, kt), kt)
            start = (tp if f == 0 else other) * half + j * kt
            a = nt_dot(bd[...], wbuf[f, 0, t, :]) * fg_ref[:, pl.ds(pl.multiple_of(start, kt), kt)]
            if f == 0:
                gq[mine_h, t] = a.astype(BF16)
            else:
                mix[mine_h, t] = a.astype(BF16)
            return c

        lax.fori_loop(0, half // kt, absorb, 0)
    send_gq = to_other(mix.at[mine_h, :], gq.at[mine_h, :], 3 + groups)
    send_gq.start()

    copy_wo.wait()

    def out_own(j, c):
        t = pl.ds(pl.multiple_of(j * nt, nt), nt)
        per = cols // nt
        acc[j // per, :, pl.ds(pl.multiple_of((j % per) * nt, nt), nt)] = nn_dot(att[...], wo[0, :, t])
        return c

    lax.fori_loop(0, half // nt, out_own, 0)
    for s in send_att:
        s.wait()
    send_gq.wait()
    send_wo.wait()
    sq[...] = jnp.zeros_like(sq)
    sc[...] = jnp.zeros_like(sc)

    def out_peer(j, c):
        t = pl.ds(pl.multiple_of(j * nt, nt), nt)
        per = cols // nt
        a = acc[j // per, :, pl.ds(pl.multiple_of((j % per) * nt, nt), nt)]
        e = (tok[:, t].astype(F32) + (a + nn_dot(attp[...], wo[1, :, t]))).astype(BF16)
        enc[:, t] = e
        wide = e.astype(F32)
        sq[...] += lane_fold(wide * wide)
        sc[...] += nt_dot(e, gq[:, t])
        return c

    lax.fori_loop(0, half // nt, out_peer, 0)
    copy_enc = pltpu.make_async_copy(enc, enc_hbm, lsem.at[13])
    send_sq2 = to_other(sq, sqp, 0)
    send_sc = to_other(sc, scp, 4 + groups)
    send_sq2.start()
    send_sc.start()
    copy_enc.start()
    send_sq2.wait()
    send_sc.wait()

    x = jnp.sum(sq[...] + sqp[...], axis=-1, keepdims=True) * (1.0 / width) + EPS
    iv = lax.rsqrt(x)
    s = (sc[...] + scp[...]) * iv * SCALE
    row = lax.broadcasted_iota(jnp.int32, (rows, 1), 0)
    limit = jnp.zeros((rows, 1), jnp.int32) + len_ref[0, psg * passages]
    for p in range(1, passages):
        limit = jnp.where(row >= p * plen, p * plen + len_ref[0, psg * passages + p], limit)
    live = row < limit
    s = jnp.where(live, s, NEGATIVE)
    peak = jnp.max(s, axis=0, keepdims=True)
    e = jnp.where(live, jnp.exp2((s - peak) * LOG2E), 0.0)
    wi = (e * iv).astype(BF16).astype(F32)
    total = jnp.sum(wi * (x * iv), axis=0, keepdims=True)
    wt = jnp.transpose(wi).astype(BF16)
    stat[0:1, :] = peak
    stat[1:2, :] = total
    stat[2:8, :] = jnp.zeros((6, 128), F32)

    def to_psg(k, src, dst, ss, rs):
        return pltpu.make_async_remote_copy(
            src_ref=src, dst_ref=dst.at[psg], send_sem=ss.at[k - 1], recv_sem=rs.at[k - 1],
            device_id={"psg": lax.rem(psg + k, npsg)}, device_id_type=MESH,
        )

    def start_stat(k, c):
        to_psg(k, stat, stats, ssend, srecv).start()
        return c

    lax.fori_loop(1, npsg, start_stat, 0)
    stats[psg] = stat[...]

    def mixed(j, c):
        t = pl.ds(pl.multiple_of(j * nt, nt), nt)
        gain = fg_ref[:, pl.ds(pl.multiple_of(tp * half + j * nt, nt), nt)]
        mix[:, t] = (nn_dot(wt, enc[:, t]) * gain).astype(BF16)
        return c

    lax.fori_loop(0, half // nt, mixed, 0)
    send_mix = to_other(mix.at[peer_h, :], mixp, 5 + groups)
    send_mix.start()

    def wait_stat(k, c):
        to_psg(k, stat, stats, ssend, srecv).wait()
        return c

    lax.fori_loop(1, npsg, wait_stat, 0)
    peaks = jnp.max(stats[:, 0:1, :], axis=0)
    totals = jnp.sum(stats[:, 1:2, :] * jnp.exp2((stats[:, 0:1, :] - peaks) * LOG2E), axis=0)
    factor = jnp.exp2((peak - peaks) * LOG2E) / totals
    sq[0:128, :] = jnp.transpose(jnp.broadcast_to(factor, (128, 128)))
    scale_col = sq[mine_h, :][:, :1]

    ct = 256
    r_head = lax.rem(lax.broadcasted_iota(jnp.int32, (hb, ct), 0), heads)
    c_head = lax.broadcasted_iota(jnp.int32, (hb, ct), 1) // DH

    copy_cv[0].wait()
    for g in range(cols // ct):
        t = slice(g * ct, (g + 1) * ct)
        acc[0, 0:hb, t] = nn_dot(mix[mine_h, :], wbuf[2, 0, :, t])
    copy_cv[1].wait()
    send_mix.wait()
    for g in range(cols // ct):
        t = slice(g * ct, (g + 1) * ct)
        m = (acc[0, 0:hb, t] + nn_dot(mixp[...], wbuf[0, 1, :, t])) * scale_col
        m = jnp.where(r_head == c_head + g * (ct // DH), m, 0.0)
        for b in range(beams):
            ctp[b : b + 1, t] = jnp.sum(m[b * heads : (b + 1) * heads], axis=0, keepdims=True)

    def start_ctx(k, c):
        to_psg(k, ctp, cts, csend, crecv).start()
        return c

    lax.fori_loop(1, npsg, start_ctx, 0)
    cts[psg] = ctp[...]

    def wait_ctx(k, c):
        to_psg(k, ctp, cts, csend, crecv).wait()
        return c

    lax.fori_loop(1, npsg, wait_ctx, 0)
    ctx_ref[...] = jnp.sum(cts[...], axis=0)
    copy_enc.wait()


def per_device(
    tokens, lengths, enc_gain, w_query, w_key, w_value, w_out, final_gain, cross_key, cross_value,
    beam_states, parents, dec_gain, dec_query,
):
    questions, passages, plen, half = tokens.shape
    rows = questions * passages * plen
    cols = w_query.shape[1]
    heads = cols // DH
    beams = beam_states.shape[1]
    hb = heads * beams
    width = 2 * half
    npsg, npb = lax.axis_size("psg"), lax.axis_size("pb")
    groups = cols // 256
    vmem = pl.BlockSpec(memory_space=pltpu.VMEM)
    smem = pl.BlockSpec(memory_space=pltpu.SMEM)
    hbm = pl.BlockSpec(memory_space=pl.ANY)
    V, D = pltpu.VMEM, pltpu.SemaphoreType.DMA
    encoded, context = pl.pallas_call(
        functools.partial(body, (npsg, npb)),
        out_shape=(
            jax.ShapeDtypeStruct((rows, half), BF16),
            jax.ShapeDtypeStruct((beams, cols), F32),
        ),
        in_specs=[hbm, smem, vmem, hbm, hbm, hbm, hbm, vmem, hbm, hbm, vmem, smem, vmem, hbm],
        out_specs=(hbm, vmem),
        scratch_shapes=[
            V((rows, half), BF16),
            V((rows, half), BF16),
            V((rows, half), BF16),
            V((3, 2, half, cols), BF16),
            V((2, cols, half), BF16),
            V((3, rows, cols), F32),
            V((3, rows, cols), BF16),
            V((rows, cols), BF16),
            V((rows, cols), BF16),
            V((rows, half), BF16),
            V((width // npb, cols), BF16),
            V((rows, 128), F32),
            V((rows, 128), F32),
            V((rows, 128), F32),
            V((2 * hb, half), BF16),
            V((rows, 2 * hb), F32),
            V((rows, 2 * hb), F32),
            V((2 * hb, half), BF16),
            V((hb, half), BF16),
            V((hb, cols), BF16),
            V((npb, 8, width // npb), F32),
            V((npb, 8, width // npb), F32),
            V((npb, 8, cols), F32),
            V((npb, 8, cols), F32),
            V((8, 2 * hb), F32),
            V((npsg, 8, 2 * hb), F32),
            V((beams, cols), F32),
            V((npsg, beams, cols), F32),
            D((14,)),
            D((6 + groups,)),
            D((6 + groups,)),
            D((2 * (npb - 1),)),
            D((2 * (npb - 1),)),
            D((npsg - 1,)),
            D((npsg - 1,)),
            D((npsg - 1,)),
            D((npsg - 1,)),
        ],
        compiler_params=pltpu.CompilerParams(
            collective_id=0, has_side_effects=True, vmem_limit_bytes=60 * 2**20
        ),
    )(
        tokens.reshape(rows, half), lengths, enc_gain.reshape(1, width), w_query, w_key, w_value, w_out,
        final_gain.reshape(1, width), cross_key, cross_value, beam_states.reshape(beams, width), parents,
        dec_gain.reshape(1, width), dec_query,
    )
    return (
        encoded.reshape(questions, passages, plen, half),
        context.reshape(questions, beams, cols),
    )


def solution(mesh):
    in_specs = (
        P("pb", "psg", None, "tp"),
        P("pb", None),
        P(),
        P(None, "tp"),
        P(None, "tp"),
        P(None, "tp"),
        P("tp", None),
        P(),
        P(None, "tp"),
        P(None, "tp"),
        P("pb", None, None),
        P("pb", None),
        P(),
        P("pb", "tp"),
    )
    out_specs = (P("pb", "psg", None, "tp"), P("pb", None, "tp"))
    return jax.shard_map(
        per_device, mesh=mesh, in_specs=in_specs, out_specs=out_specs, check_vma=False
    )
```

time: 318 us -> 62.2 us (0.20)
  blocking collectives: 154 us -> 0 us
  Pallas kernels: 0 us -> 56.8 us
  matrix products: 52.4 us -> 0 us
  local copies, waits for them, and re-layouts: 42.8 us -> 4.48 us
  waiting for transfers between devices: 33.2 us -> 0 us
  other arithmetic: 16 us -> 0 us
  between operations: 14.7 us -> 0.64 us
  starting transfers between devices: 3.6 us -> 0 us
    psum x2 -> x0, blocking collectives: 72.1 us -> none  [the longest x1 69.5 us: per_device(): joined = lax.psum(joined, 'psg')]
    pallas_call x0 -> x1, Pallas kernels: none -> 56.8 us  [per_device(): pl.pallas_call(functools.partial(body, (npsg, npb)), out_shape=(jax.Shape...]
    dot_general x12 -> x0, matrix products: 52.4 us -> none  [the longest x3 21.9 us: project(): product = jnp.dot(normed, matrix, preferred_element_type=jnp.float32)]
    pmax x1 -> x0, blocking collectives: 41 us -> none  [per_device(): whole_peak = lax.pmax(my_peak, 'psg')]
    unnamed x27 -> x2, local copies, waits for them, and re-layouts: 27.4 us -> 4.48 us
    all_gather x2 -> x0, blocking collectives: 21.9 us -> none  [the longest x1 12 us: per_device(): all_states = lax.all_gather(beam_states, 'pb', axis=0, tiled=True)]
    all_gather x1 -> x0, waiting for transfers between devices: 19.7 us -> none  [per_device(): lax.all_gather(tokens, 'tp', axis=3, tiled=True).reshape(rows, model_width)]
    unnamed x1 -> x0, blocking collectives: 14.8 us -> none
  transfers between devices with their start and end apart: 4 -> 0, of which waited for: 2 -> 0; matrix products, arithmetic and copies ran while one was open for 11% -> 0% of each run, Pallas kernels for 0% -> 0%
where the time goes in v2:
time: 62.2 us; the launch traced here: 61.9 us
  Pallas kernels  56.8 us (91%)
  local copies, waits for them, and re-layouts  4.48 us (7%)
  between operations  0.64 us (1%)
    pallas_call x1, Pallas kernels, per_device(): pl.pallas_call(functools.partial(body, (npsg, npb)), out_shape=(jax.Shape...  56.8 us
    unnamed x2, local copies, waits for them, and re-layouts  4.48 us

profile of v2, /device:TPU:0, one launch (start us, length us, event | category | flops | bytes accessed | tf_op | source)
XLA Modules:
  0.0 61.9 jit_solution(8985257675074682012)
XLA Ops:
  0.6 56.8 %shard_map.149 = (bf16[512,2048]{1,0:T(8,128)(2,1)}, f32[4,1024]{1,0:T(4,128)}) custom-call(bf16[512,2048]{1,0:T(8,128)(2,1)} %bitcast.7, s32[1,32]{1,0:T(1,128)} %len_ref.1, f32[1,4096]{1,0:T(1,128)} %bitcast.10, bf16[4096,1024]{1,0:T(8,128)(2,1)} %wq_hbm.1, bf16[4096,1024]{1,0:T(8,128)(2,1)} %wk_hbm.1, bf16[4096,1024]{1,0:T(8,128)(2,1)} %wv_hbm.1, ...), custom_call_target="tpu_custom_call" | custom-call | tf_op jit(solution)/shard_map/pallas_call | solution.py:401
  57.4 3.2 %copy.18 = bf16[1,2,256,2048]{3,2,1,0:T(8,128)(2,1)} copy(bf16[1,2,256,2048]{3,2,1,0:T(8,128)(2,1)} %bitcast.8) | data formatting | bytes 4194304
  60.6 1.3 %copy.19 = f32[1,4,1024]{2,1,0:T(4,128)} copy(f32[1,4,1024]{2,1,0:T(4,128)} %bitcast.13) | data formatting | bytes 32768

commit v3 on v2

--- a/solution.py
+++ b/solution.py
@@ -102,13 +102,14 @@
     blk = 32
     copy_tok.wait()
 
-    def squares(i, c):
+    def scale_local(i, c):
         r = pl.ds(pl.multiple_of(i * blk, blk), blk)
         x = tok[r, :].astype(F32)
         sq[r, :] = lane_fold(x * x)
-        return c
-
-    lax.fori_loop(0, rows // blk, squares, 0)
+        xl[r, :] = (x * eg_ref[:, mine_f]).astype(BF16)
+        return c
+
+    lax.fori_loop(0, rows // blk, scale_local, 0)
 
     pl.semaphore_wait(barrier, npsg - 1 + npb - 1 + 1)
 
@@ -119,10 +120,10 @@
         )
 
     send_sq = to_other(sq, sqp, 0)
-    send_tok = to_other(tok, xr, 1)
+    send_tok = to_other(xl, xr, 1)
     send_wo = to_other(wo_hbm.at[:, peer_f], wo.at[1], 2)
+    send_tok.start()
     send_sq.start()
-    send_tok.start()
 
     def to_pb(k, src, dst, base):
         to = lax.rem(pb + k, npb)
@@ -135,19 +136,6 @@
     for s in send_dn:
         s.start()
     dnr[pb] = dn[pb]
-
-    send_sq.wait()
-
-    def normalise_local(i, c):
-        r = pl.ds(pl.multiple_of(i * blk, blk), blk)
-        ms = jnp.sum(sq[r, :] + sqp[r, :], axis=-1, keepdims=True) * (1.0 / width) + EPS
-        v = jnp.broadcast_to(lax.rsqrt(ms), (blk, 128))
-        inv[r, :] = v
-        x = tok[r, :].astype(F32)
-        xl[r, :] = (x * v[:, :1] * eg_ref[:, mine_f]).astype(BF16)
-        return c
-
-    lax.fori_loop(0, rows // blk, normalise_local, 0)
 
     nt = min(512, cols)
     for w in range(3):
@@ -183,21 +171,23 @@
 
     send_tok.wait()
     send_wo.start()
-
-    def normalise_peer(i, c):
+    send_sq.wait()
+
+    def inverse(i, c):
         r = pl.ds(pl.multiple_of(i * blk, blk), blk)
-        x = xr[r, :].astype(F32)
-        xr[r, :] = (x * inv[r, :1] * eg_ref[:, peer_f]).astype(BF16)
-        return c
-
-    lax.fori_loop(0, rows // blk, normalise_peer, 0)
+        ms = jnp.sum(sq[r, :] + sqp[r, :], axis=-1, keepdims=True) * (1.0 / width) + EPS
+        inv[r, :] = jnp.broadcast_to(lax.rsqrt(ms), (blk, 128))
+        return c
+
+    lax.fori_loop(0, rows // blk, inverse, 0)
 
     for w in range(3):
         copy_w[w][1].wait()
 
         def second_half(j, c):
             t = pl.ds(pl.multiple_of(j * nt, nt), nt)
-            qkv[w, :, t] = (acc[w, :, t] + nn_dot(xr[...], wbuf[w, 1, :, t])).astype(BF16)
+            scale = jnp.concatenate([inv[...]] * (nt // 128), axis=1)
+            qkv[w, :, t] = ((acc[w, :, t] + nn_dot(xr[...], wbuf[w, 1, :, t])) * scale).astype(BF16)
             return c
 
         lax.fori_loop(0, cols // nt, second_half, 0)
@@ -273,7 +263,7 @@
     send_gq.wait()
     send_wo.wait()
     sq[...] = jnp.zeros_like(sq)
-    sc[...] = jnp.zeros_like(sc)
+    sc[0 : 2 * hb, :] = jnp.zeros((2 * hb, rows), F32)
 
     def out_peer(j, c):
         t = pl.ds(pl.multiple_of(j * nt, nt), nt)
@@ -283,36 +273,30 @@
         enc[:, t] = e
         wide = e.astype(F32)
         sq[...] += lane_fold(wide * wide)
-        sc[...] += nt_dot(e, gq[:, t])
+        sc[0 : 2 * hb, :] += nt_dot(gq[:, t], e)
         return c
 
     lax.fori_loop(0, half // nt, out_peer, 0)
     copy_enc = pltpu.make_async_copy(enc, enc_hbm, lsem.at[13])
-    send_sq2 = to_other(sq, sqp, 0)
+    sc[2 * hb : 2 * hb + 8, :] = jnp.broadcast_to(jnp.sum(jnp.transpose(sq[...]), axis=0, keepdims=True), (8, rows))
     send_sc = to_other(sc, scp, 4 + groups)
-    send_sq2.start()
     send_sc.start()
     copy_enc.start()
-    send_sq2.wait()
     send_sc.wait()
 
-    x = jnp.sum(sq[...] + sqp[...], axis=-1, keepdims=True) * (1.0 / width) + EPS
+    both = sc[...] + scp[...]
+    x = both[2 * hb : 2 * hb + 1, :] * (1.0 / width) + EPS
     iv = lax.rsqrt(x)
-    s = (sc[...] + scp[...]) * iv * SCALE
-    row = lax.broadcasted_iota(jnp.int32, (rows, 1), 0)
-    limit = jnp.zeros((rows, 1), jnp.int32) + len_ref[0, psg * passages]
+    at = lax.broadcasted_iota(jnp.int32, (1, rows), 1)
+    limit = jnp.zeros((1, rows), jnp.int32) + len_ref[0, psg * passages]
     for p in range(1, passages):
-        limit = jnp.where(row >= p * plen, p * plen + len_ref[0, psg * passages + p], limit)
-    live = row < limit
-    s = jnp.where(live, s, NEGATIVE)
-    peak = jnp.max(s, axis=0, keepdims=True)
+        limit = jnp.where(at >= p * plen, p * plen + len_ref[0, psg * passages + p], limit)
+    live = at < limit
+    s = jnp.where(live, both[0 : 2 * hb, :] * (iv * SCALE), NEGATIVE)
+    peak = jnp.max(s, axis=1, keepdims=True)
     e = jnp.where(live, jnp.exp2((s - peak) * LOG2E), 0.0)
-    wi = (e * iv).astype(BF16).astype(F32)
-    total = jnp.sum(wi * (x * iv), axis=0, keepdims=True)
-    wt = jnp.transpose(wi).astype(BF16)
-    stat[0:1, :] = peak
-    stat[1:2, :] = total
-    stat[2:8, :] = jnp.zeros((6, 128), F32)
+    wt = (e * iv).astype(BF16)
+    total = jnp.sum(wt.astype(F32) * (x * iv), axis=1, keepdims=True)
 
     def to_psg(k, src, dst, ss, rs):
         return pltpu.make_async_remote_copy(
@@ -320,13 +304,6 @@
             device_id={"psg": lax.rem(psg + k, npsg)}, device_id_type=MESH,
         )
 
-    def start_stat(k, c):
-        to_psg(k, stat, stats, ssend, srecv).start()
-        return c
-
-    lax.fori_loop(1, npsg, start_stat, 0)
-    stats[psg] = stat[...]
-
     def mixed(j, c):
         t = pl.ds(pl.multiple_of(j * nt, nt), nt)
         gain = fg_ref[:, pl.ds(pl.multiple_of(tp * half + j * nt, nt), nt)]
@@ -336,17 +313,16 @@
     lax.fori_loop(0, half // nt, mixed, 0)
     send_mix = to_other(mix.at[peer_h, :], mixp, 5 + groups)
     send_mix.start()
-
-    def wait_stat(k, c):
-        to_psg(k, stat, stats, ssend, srecv).wait()
-        return c
-
-    lax.fori_loop(1, npsg, wait_stat, 0)
-    peaks = jnp.max(stats[:, 0:1, :], axis=0)
-    totals = jnp.sum(stats[:, 1:2, :] * jnp.exp2((stats[:, 0:1, :] - peaks) * LOG2E), axis=0)
-    factor = jnp.exp2((peak - peaks) * LOG2E) / totals
-    sq[0:128, :] = jnp.transpose(jnp.broadcast_to(factor, (128, 128)))
-    scale_col = sq[mine_h, :][:, :1]
+    first = lax.broadcasted_iota(jnp.int32, (2 * hb, 128), 1) == 0
+    stat[...] = jnp.transpose(jnp.where(first, peak, total))[0:8, :]
+
+    def start_stat(k, c):
+        to_psg(k, stat, stats, ssend, srecv).start()
+        return c
+
+    lax.fori_loop(1, npsg, start_stat, 0)
+    stats[psg] = stat[...]
+
 
     ct = 256
     r_head = lax.rem(lax.broadcasted_iota(jnp.int32, (hb, ct), 0), heads)
@@ -356,6 +332,17 @@
     for g in range(cols // ct):
         t = slice(g * ct, (g + 1) * ct)
         acc[0, 0:hb, t] = nn_dot(mix[mine_h, :], wbuf[2, 0, :, t])
+    def wait_stat(k, c):
+        to_psg(k, stat, stats, ssend, srecv).wait()
+        return c
+
+    lax.fori_loop(1, npsg, wait_stat, 0)
+    peaks = jnp.max(stats[:, 0:1, :], axis=0)
+    totals = jnp.sum(stats[:, 1:2, :] * jnp.exp2((stats[:, 0:1, :] - peaks) * LOG2E), axis=0)
+    factor = jnp.exp2((stat[0:1, :] - peaks) * LOG2E) / totals
+    sq[0:128, :] = jnp.transpose(jnp.broadcast_to(factor, (128, 128)))
+    scale_col = sq[mine_h, :][:, :1]
+
     copy_cv[1].wait()
     send_mix.wait()
     for g in range(cols // ct):
@@ -379,6 +366,20 @@
     lax.fori_loop(1, npsg, wait_ctx, 0)
     ctx_ref[...] = jnp.sum(cts[...], axis=0)
     copy_enc.wait()
+
+
+def writer(enc_hbm, ctx_hbm, enc_out, ctx_out, sem):
+    n = sem.shape[0] - 1
+    rows = enc_hbm.shape[0] // n
+    copies = [
+        pltpu.make_async_copy(enc_hbm.at[pl.ds(i * rows, rows), :], enc_out.at[pl.ds(i * rows, rows), :], sem.at[i])
+        for i in range(n)
+    ]
+    copies.append(pltpu.make_async_copy(ctx_hbm, ctx_out, sem.at[n]))
+    for c in copies:
+        c.start()
+    for c in copies:
+        c.wait()
 
 
 def per_device(
@@ -422,8 +423,8 @@
             V((rows, 128), F32),
             V((rows, 128), F32),
             V((2 * hb, half), BF16),
-            V((rows, 2 * hb), F32),
-            V((rows, 2 * hb), F32),
+            V((2 * hb + 8, rows), F32),
+            V((2 * hb + 8, rows), F32),
             V((2 * hb, half), BF16),
             V((hb, half), BF16),
             V((hb, cols), BF16),
@@ -453,6 +454,16 @@
         final_gain.reshape(1, width), cross_key, cross_value, beam_states.reshape(beams, width), parents,
         dec_gain.reshape(1, width), dec_query,
     )
+    encoded, context = pl.pallas_call(
+        writer,
+        out_shape=(
+            jax.ShapeDtypeStruct((rows, half), BF16),
+            jax.ShapeDtypeStruct((beams, cols), F32),
+        ),
+        in_specs=[hbm, hbm],
+        out_specs=(hbm, hbm),
+        scratch_shapes=[D((9,))],
+    )(encoded, context)
     return (
         encoded.reshape(questions, passages, plen, half),
         context.reshape(questions, beams, cols),

time: 62.2 us -> 120 us (1.93)
  Pallas kernels: 56.8 us -> 119 us
  local copies, waits for them, and re-layouts: 4.48 us -> 0 us
    pallas_call x0 -> x1, Pallas kernels: none -> 65.2 us  [per_device(): pl.pallas_call(writer, out_shape=(jax.ShapeDtypeStruct((rows, half), BF16...]
    unnamed x2 -> x0, local copies, waits for them, and re-layouts: 4.48 us -> none
    pallas_call x1, Pallas kernels: 56.8 us -> 53.9 us  [per_device(): pl.pallas_call(functools.partial(body, (npsg, npb)), out_shape=(jax.Shape...]
where the time goes in v3:
time: 120 us
  Pallas kernels  119 us (99%)
    pallas_call x1, Pallas kernels, per_device(): pl.pallas_call(writer, out_shape=(jax.ShapeDtypeStruct((rows, half), BF16...  65.2 us
    pallas_call x1, Pallas kernels, per_device(): pl.pallas_call(functools.partial(body, (npsg, npb)), out_shape=(jax.Shape...  53.9 us

profile of v3, /device:TPU:0, one launch (start us, length us, event | category | flops | bytes accessed | tf_op | source)
XLA Modules:
  0.0 119.7 jit_solution(14282386800520195307)
XLA Ops:
  0.6 53.9 %shard_map.149 = (bf16[512,2048]{1,0:T(8,128)(2,1)}, f32[4,1024]{1,0:T(4,128)}) custom-call(bf16[512,2048]{1,0:T(8,128)(2,1)} %bitcast.7, s32[1,32]{1,0:T(1,128)} %len_ref.1, f32[1,4096]{1,0:T(1,128)} %bitcast.9, bf16[4096,1024]{1,0:T(8,128)(2,1)} %wq_hbm.1, bf16[4096,1024]{1,0:T(8,128)(2,1)} %wk_hbm.1, bf16[4096,1024]{1,0:T(8,128)(2,1)} %wv_hbm.1, ...), custom_call_target="tpu_custom_call" | custom-call | tf_op jit(solution)/shard_map/pallas_call | solution.py:402
  54.5 65.2 %shard_map.150 = (bf16[512,2048]{1,0:T(8,128)(2,1)}, f32[4,1024]{1,0:T(4,128)}) custom-call(bf16[512,2048]{1,0:T(8,128)(2,1)} %get-tuple-element.6.enc_hbm, f32[4,1024]{1,0:T(4,128)} %get-tuple-element.7.ctx_hbm), custom_call_target="tpu_custom_call" | custom-call | tf_op jit(solution)/shard_map/pallas_call | solution.py:457

commit v4 on v3

--- a/solution.py
+++ b/solution.py
@@ -37,8 +37,8 @@
     tok_hbm, len_ref, eg_ref, wq_hbm, wk_hbm, wv_hbm, wo_hbm, fg_ref, ck_hbm, cv_hbm, beam_ref, par_ref, dg_ref, dec_hbm,
     enc_hbm, ctx_ref,
     tok, xl, xr, wbuf, wo, acc, qkv, att, attp, enc, decw,
-    sq, sqp, inv, gq, sc, scp, mix, mixp, bd, dn, dnr, dqp, dqr, stat, stats, ctp, cts,
-    lsem, tsend, trecv, psend, precv, ssend, srecv, csend, crecv,
+    sq, sqp, inv, gq, sc, scp, mix, mixp, bd, dn, dnr, dqp, dqr, stat, stats, ctf, ctp, cts, xs, ckb, gpart, gqa, gqp,
+    lsem, tsend, trecv, psend, precv, ssend, srecv, csend, crecv, gsend, grecv,
 ):
     npsg, npb = sizes
     rows, half = tok.shape
@@ -67,8 +67,14 @@
     for k in range(1, npb):
         pl.semaphore_signal(barrier, inc=1, device_id={"pb": lax.rem(pb + k, npb)}, device_id_type=MESH)
 
-    copy_tok = pltpu.make_async_copy(tok_hbm, tok, lsem.at[0])
-    copy_tok.start()
+    parts = 4
+    prow = rows // parts
+    copy_tok = [
+        pltpu.make_async_copy(tok_hbm.at[pl.ds(i * prow, prow), :], tok.at[pl.ds(i * prow, prow), :], lsem.at[10 + i])
+        for i in range(parts)
+    ]
+    for c in copy_tok:
+        c.start()
     w_hbm = (wq_hbm, wk_hbm, wv_hbm)
     copy_w = [[None, None] for _ in range(3)]
     for h, part in enumerate((mine_f, peer_f)):
@@ -79,6 +85,13 @@
     for w in range(3):
         copy_w[w][0].start()
     copy_dec.start()
+    fc = half // npsg
+    copy_ck = [
+        pltpu.make_async_copy(ck_hbm.at[pl.ds(pl.multiple_of(c * half + psg * fc, fc), fc), :], ckb.at[f], lsem.at[14 + f])
+        for f, c in enumerate((tp, other))
+    ]
+    for c in copy_ck:
+        c.start()
     for w in range(3):
         copy_w[w][1].start()
     copy_wo.start()
@@ -100,7 +113,6 @@
         dn[j, beams:8, :] = jnp.zeros((8 - beams, depth), F32)
 
     blk = 32
-    copy_tok.wait()
 
     def scale_local(i, c):
         r = pl.ds(pl.multiple_of(i * blk, blk), blk)
@@ -109,7 +121,9 @@
         xl[r, :] = (x * eg_ref[:, mine_f]).astype(BF16)
         return c
 
-    lax.fori_loop(0, rows // blk, scale_local, 0)
+    for i in range(parts):
+        copy_tok[i].wait()
+        lax.fori_loop(i * prow // blk, (i + 1) * prow // blk, scale_local, 0)
 
     pl.semaphore_wait(barrier, npsg - 1 + npb - 1 + 1)
 
@@ -132,6 +146,12 @@
             device_id={"pb": to}, device_id_type=MESH,
         )
 
+    def to_psg(k, src, dst, ss, rs):
+        return pltpu.make_async_remote_copy(
+            src_ref=src, dst_ref=dst, send_sem=ss.at[k - 1], recv_sem=rs.at[k - 1],
+            device_id={"psg": lax.rem(psg + k, npsg)}, device_id_type=MESH,
+        )
+
     send_dn = [to_pb(k, dn, dnr, 0) for k in range(1, npb)]
     for s in send_dn:
         s.start()
@@ -147,28 +167,20 @@
             return c
 
         lax.fori_loop(0, cols // nt, first_half, 0)
-
-    copy_ck = [
-        pltpu.make_async_copy(ck_hbm.at[mine_f, :], wbuf.at[0, 0], lsem.at[9]),
-        pltpu.make_async_copy(ck_hbm.at[peer_f, :], wbuf.at[1, 0], lsem.at[10]),
+        if w == 1:
+            for s in send_dn:
+                s.wait()
+            copy_dec.wait()
+            dqp[...] = nn_dot(dnr[...].reshape(npb * 8, depth).astype(BF16), decw[...]).reshape(npb, 8, cols)
+            send_dq = [to_pb(k, dqp, dqr, npb - 1) for k in range(1, npb)]
+            for s in send_dq:
+                s.start()
+            dqr[pb] = dqp[pb]
+
+    copy_cv = [
+        pltpu.make_async_copy(cv_hbm.at[mine_f, :], wbuf.at[0, 0], lsem.at[0]),
+        pltpu.make_async_copy(cv_hbm.at[peer_f, :], wbuf.at[1, 0], lsem.at[9]),
     ]
-    copy_cv = [
-        pltpu.make_async_copy(cv_hbm.at[mine_f, :], wbuf.at[2, 0], lsem.at[11]),
-        pltpu.make_async_copy(cv_hbm.at[peer_f, :], wbuf.at[0, 1], lsem.at[12]),
-    ]
-    copy_ck[0].start()
-    copy_ck[1].start()
-    copy_cv[0].start()
-
-    for s in send_dn:
-        s.wait()
-    copy_dec.wait()
-    dqp[...] = nn_dot(dnr[...].reshape(npb * 8, depth).astype(BF16), decw[...]).reshape(npb, 8, cols)
-    send_dq = [to_pb(k, dqp, dqr, npb - 1) for k in range(1, npb)]
-    for s in send_dq:
-        s.start()
-    dqr[pb] = dqp[pb]
-
     send_tok.wait()
     send_wo.start()
     send_sq.wait()
@@ -192,7 +204,29 @@
 
         lax.fori_loop(0, cols // nt, second_half, 0)
         if w == 0:
+            copy_cv[0].start()
             copy_cv[1].start()
+            for s in send_dq:
+                s.wait()
+            dq = dqr[0]
+            for j in range(1, npb):
+                dq = dq + dqr[j]
+            dq = dq.astype(BF16).astype(F32)
+            head_of = lax.broadcasted_iota(jnp.int32, (heads, cols), 1) // DH
+            head_row = lax.broadcasted_iota(jnp.int32, (heads, cols), 0)
+            for b in range(beams):
+                bd[b * heads : (b + 1) * heads, :] = jnp.where(head_of == head_row, dq[b : b + 1, :], 0.0).astype(BF16)
+            for f, c in enumerate((tp, other)):
+                copy_ck[f].wait()
+                gain = fg_ref[:, pl.ds(pl.multiple_of(c * half + psg * fc, fc), fc)]
+                gpart[f] = (nt_dot(bd[...], ckb[f]) * gain).astype(BF16)
+
+            def start_gq(k, c):
+                to_psg(k, gpart, gqa.at[:, psg], gsend, grecv).start()
+                return c
+
+            lax.fori_loop(1, npsg, start_gq, 0)
+            gqa[:, psg] = gpart[...]
 
     lane = lax.broadcasted_iota(jnp.int32, (plen, 128), 1)
     low = lane < DH
@@ -218,36 +252,18 @@
         s.start()
         send_att.append(s)
 
-    for s in send_dq:
-        s.wait()
-    dq = dqr[0]
-    for j in range(1, npb):
-        dq = dq + dqr[j]
-    dq = dq.astype(BF16).astype(F32)
-    head_of = lax.broadcasted_iota(jnp.int32, (heads, cols), 1) // DH
-    head_row = lax.broadcasted_iota(jnp.int32, (heads, cols), 0)
-    for b in range(beams):
-        bd[b * heads : (b + 1) * heads, :] = jnp.where(head_of == head_row, dq[b : b + 1, :], 0.0).astype(BF16)
     mine_h = pl.ds(pl.multiple_of(tp * hb, hb), hb)
     peer_h = pl.ds(pl.multiple_of(other * hb, hb), hb)
-    kt = min(512, half)
-
-    for f in range(2):
-        copy_ck[f].wait()
-
-        def absorb(j, c):
-            t = pl.ds(pl.multiple_of(j * kt, kt), kt)
-            start = (tp if f == 0 else other) * half + j * kt
-            a = nt_dot(bd[...], wbuf[f, 0, t, :]) * fg_ref[:, pl.ds(pl.multiple_of(start, kt), kt)]
-            if f == 0:
-                gq[mine_h, t] = a.astype(BF16)
-            else:
-                mix[mine_h, t] = a.astype(BF16)
-            return c
-
-        lax.fori_loop(0, half // kt, absorb, 0)
-    send_gq = to_other(mix.at[mine_h, :], gq.at[mine_h, :], 3 + groups)
+
+    def wait_gq(k, c):
+        to_psg(k, gpart, gqa.at[:, psg], gsend, grecv).wait()
+        return c
+
+    lax.fori_loop(1, npsg, wait_gq, 0)
+    send_gq = to_other(gqa.at[1], gqp, 3 + groups)
     send_gq.start()
+    for i in range(npsg):
+        gq[mine_h, i * fc : (i + 1) * fc] = gqa[0, i]
 
     copy_wo.wait()
 
@@ -261,6 +277,8 @@
     for s in send_att:
         s.wait()
     send_gq.wait()
+    for i in range(npsg):
+        gq[peer_h, i * fc : (i + 1) * fc] = gqp[i]
     send_wo.wait()
     sq[...] = jnp.zeros_like(sq)
     sc[0 : 2 * hb, :] = jnp.zeros((2 * hb, rows), F32)
@@ -298,12 +316,6 @@
     wt = (e * iv).astype(BF16)
     total = jnp.sum(wt.astype(F32) * (x * iv), axis=1, keepdims=True)
 
-    def to_psg(k, src, dst, ss, rs):
-        return pltpu.make_async_remote_copy(
-            src_ref=src, dst_ref=dst.at[psg], send_sem=ss.at[k - 1], recv_sem=rs.at[k - 1],
-            device_id={"psg": lax.rem(psg + k, npsg)}, device_id_type=MESH,
-        )
-
     def mixed(j, c):
         t = pl.ds(pl.multiple_of(j * nt, nt), nt)
         gain = fg_ref[:, pl.ds(pl.multiple_of(tp * half + j * nt, nt), nt)]
@@ -317,7 +329,7 @@
     stat[...] = jnp.transpose(jnp.where(first, peak, total))[0:8, :]
 
     def start_stat(k, c):
-        to_psg(k, stat, stats, ssend, srecv).start()
+        to_psg(k, stat, stats.at[psg], ssend, srecv).start()
         return c
 
     lax.fori_loop(1, npsg, start_stat, 0)
@@ -331,54 +343,71 @@
     copy_cv[0].wait()
     for g in range(cols // ct):
         t = slice(g * ct, (g + 1) * ct)
-        acc[0, 0:hb, t] = nn_dot(mix[mine_h, :], wbuf[2, 0, :, t])
-    def wait_stat(k, c):
-        to_psg(k, stat, stats, ssend, srecv).wait()
-        return c
-
-    lax.fori_loop(1, npsg, wait_stat, 0)
-    peaks = jnp.max(stats[:, 0:1, :], axis=0)
-    totals = jnp.sum(stats[:, 1:2, :] * jnp.exp2((stats[:, 0:1, :] - peaks) * LOG2E), axis=0)
-    factor = jnp.exp2((stat[0:1, :] - peaks) * LOG2E) / totals
-    sq[0:128, :] = jnp.transpose(jnp.broadcast_to(factor, (128, 128)))
-    scale_col = sq[mine_h, :][:, :1]
-
+        acc[0, 0:hb, t] = nn_dot(mix[mine_h, :], wbuf[0, 0, :, t])
     copy_cv[1].wait()
     send_mix.wait()
     for g in range(cols // ct):
         t = slice(g * ct, (g + 1) * ct)
-        m = (acc[0, 0:hb, t] + nn_dot(mixp[...], wbuf[0, 1, :, t])) * scale_col
+        m = acc[0, 0:hb, t] + nn_dot(mixp[...], wbuf[1, 0, :, t])
         m = jnp.where(r_head == c_head + g * (ct // DH), m, 0.0)
         for b in range(beams):
-            ctp[b : b + 1, t] = jnp.sum(m[b * heads : (b + 1) * heads], axis=0, keepdims=True)
+            r = g * beams + b
+            ctf[r : r + 1, :] = jnp.sum(m[b * heads : (b + 1) * heads], axis=0, keepdims=True)
+    ctp[...] = ctf[...].astype(BF16)
 
     def start_ctx(k, c):
-        to_psg(k, ctp, cts, csend, crecv).start()
+        to_psg(k, ctp, cts.at[psg], csend, crecv).start()
         return c
 
     lax.fori_loop(1, npsg, start_ctx, 0)
     cts[psg] = ctp[...]
 
+    def wait_stat(k, c):
+        to_psg(k, stat, stats.at[psg], ssend, srecv).wait()
+        return c
+
+    lax.fori_loop(1, npsg, wait_stat, 0)
+    peaks = stats[:, 0:1, :]
+    factor = jnp.exp2((peaks - jnp.max(peaks, axis=0, keepdims=True)) * LOG2E)
+    factor = factor / jnp.sum(stats[:, 1:2, :] * factor, axis=0, keepdims=True)
+    nr = beams * cols // ct
+    per = ct // DH
+    c_of = lax.broadcasted_iota(jnp.int32, (nr, 2 * hb), 1) - tp * hb
+    r_of = lax.broadcasted_iota(jnp.int32, (nr, 2 * hb), 0)
+    own = (c_of >= 0) & (c_of < hb) & (lax.div(c_of, heads) == lax.rem(r_of, beams))
+    own = own & (lax.div(lax.rem(c_of, heads), per) == lax.div(r_of, beams))
+    own = jnp.where(own, 1.0, 0.0)
+    spread = (factor * own[None]).reshape(npsg * nr, 2 * hb)
+    coarse = spread.astype(BF16)
+    fine = (spread - coarse.astype(F32)).astype(BF16)
+    one = lax.rem(lax.broadcasted_iota(jnp.int32, (2 * hb, ct), 0), per) == lax.broadcasted_iota(jnp.int32, (2 * hb, ct), 1) // DH
+    one = jnp.where(one, 1.0, 0.0).astype(BF16)
+    xs[...] = (nn_dot(coarse, one) + nn_dot(fine, one)).reshape(npsg, nr, ct)
+
     def wait_ctx(k, c):
-        to_psg(k, ctp, cts, csend, crecv).wait()
+        to_psg(k, ctp, cts.at[psg], csend, crecv).wait()
         return c
 
     lax.fori_loop(1, npsg, wait_ctx, 0)
-    ctx_ref[...] = jnp.sum(cts[...], axis=0)
+    whole = jnp.sum(cts[...].astype(F32) * xs[...], axis=0)
+    for g in range(cols // ct):
+        ctx_ref[:, g * ct : (g + 1) * ct] = whole[g * beams : (g + 1) * beams, :]
     copy_enc.wait()
 
 
-def writer(enc_hbm, ctx_hbm, enc_out, ctx_out, sem):
-    n = sem.shape[0] - 1
+def writer(enc_hbm, ctx_in, enc_out, ctx_out, held, sem_in, sem_out):
+    n = sem_in.shape[0]
     rows = enc_hbm.shape[0] // n
-    copies = [
-        pltpu.make_async_copy(enc_hbm.at[pl.ds(i * rows, rows), :], enc_out.at[pl.ds(i * rows, rows), :], sem.at[i])
-        for i in range(n)
-    ]
-    copies.append(pltpu.make_async_copy(ctx_hbm, ctx_out, sem.at[n]))
-    for c in copies:
+    part = [pl.ds(i * rows, rows) for i in range(n)]
+    ins = [pltpu.make_async_copy(enc_hbm.at[p, :], held.at[p, :], sem_in.at[i]) for i, p in enumerate(part)]
+    outs = [pltpu.make_async_copy(held.at[p, :], enc_out.at[p, :], sem_out.at[i]) for i, p in enumerate(part)]
+    for c in ins:
         c.start()
-    for c in copies:
+    ctx_out[...] = ctx_in[...]
+    for i in range(n):
+        ins[i].wait()
+        outs[i].start()
+    for c in outs:
         c.wait()
 
 
@@ -434,13 +463,21 @@
             V((npb, 8, cols), F32),
             V((8, 2 * hb), F32),
             V((npsg, 8, 2 * hb), F32),
-            V((beams, cols), F32),
-            V((npsg, beams, cols), F32),
-            D((14,)),
+            V((beams * cols // 256, 256), F32),
+            V((beams * cols // 256, 256), BF16),
+            V((npsg, beams * cols // 256, 256), BF16),
+            V((npsg, beams * cols // 256, 256), F32),
+            V((2, half // npsg, cols), BF16),
+            V((2, hb, half // npsg), BF16),
+            V((2, npsg, hb, half // npsg), BF16),
+            V((npsg, hb, half // npsg), BF16),
+            D((16,)),
             D((6 + groups,)),
             D((6 + groups,)),
             D((2 * (npb - 1),)),
             D((2 * (npb - 1),)),
+            D((npsg - 1,)),
+            D((npsg - 1,)),
             D((npsg - 1,)),
             D((npsg - 1,)),
             D((npsg - 1,)),
@@ -460,9 +497,9 @@
             jax.ShapeDtypeStruct((rows, half), BF16),
             jax.ShapeDtypeStruct((beams, cols), F32),
         ),
-        in_specs=[hbm, hbm],
-        out_specs=(hbm, hbm),
-        scratch_shapes=[D((9,))],
+        in_specs=[hbm, vmem],
+        out_specs=(hbm, vmem),
+        scratch_shapes=[V((rows, half), BF16), D((8,)), D((8,))],
     )(encoded, context)
     return (
         encoded.reshape(questions, passages, plen, half),

time: 120 us -> 53 us (0.44)
  Pallas kernels: 119 us -> 52 us
    pallas_call x1, Pallas kernels: 65.2 us -> 3.72 us  [per_device(): pl.pallas_call(writer, out_shape=(jax.ShapeDtypeStruct((rows, half), BF16...]
    pallas_call x1, Pallas kernels: 53.9 us -> 48.3 us  [per_device(): pl.pallas_call(functools.partial(body, (npsg, npb)), out_shape=(jax.Shape...]
where the time goes in v4:
time: 53 us; the launch traced here: 52.6 us
  Pallas kernels  52 us (98%)
  between operations  0.64 us (1%)
    pallas_call x1, Pallas kernels, per_device(): pl.pallas_call(functools.partial(body, (npsg, npb)), out_shape=(jax.Shape...  48.3 us
    pallas_call x1, Pallas kernels, per_device(): pl.pallas_call(writer, out_shape=(jax.ShapeDtypeStruct((rows, half), BF16...  3.72 us

profile of v4, /device:TPU:0, one launch (start us, length us, event | category | flops | bytes accessed | tf_op | source)
XLA Modules:
  0.0 52.6 jit_solution(9166311182227430709)
XLA Ops:
  0.6 48.3 %shard_map.149 = (bf16[512,2048]{1,0:T(8,128)(2,1)}, f32[4,1024]{1,0:T(4,128)}) custom-call(bf16[512,2048]{1,0:T(8,128)(2,1)} %bitcast.7, s32[1,32]{1,0:T(1,128)} %len_ref.1, f32[1,4096]{1,0:T(1,128)} %bitcast.9, bf16[4096,1024]{1,0:T(8,128)(2,1)} %wq_hbm.1, bf16[4096,1024]{1,0:T(8,128)(2,1)} %wk_hbm.1, bf16[4096,1024]{1,0:T(8,128)(2,1)} %wv_hbm.1, ...), custom_call_target="tpu_custom_call" | custom-call | tf_op jit(solution)/shard_map/pallas_call | solution.py:431
  48.9 3.7 %shard_map.150 = (bf16[512,2048]{1,0:T(8,128)(2,1)}, f32[4,1024]{1,0:T(4,128)}) custom-call(bf16[512,2048]{1,0:T(8,128)(2,1)} %get-tuple-element.6.enc_hbm, f32[4,1024]{1,0:T(4,128)} %get-tuple-element.7.ctx_in), custom_call_target="tpu_custom_call" | custom-call | tf_op jit(solution)/shard_map/pallas_call | solution.py:494

commit v5 on v4

--- a/solution.py
+++ b/solution.py
@@ -36,11 +36,12 @@
     sizes,
     tok_hbm, len_ref, eg_ref, wq_hbm, wk_hbm, wv_hbm, wo_hbm, fg_ref, ck_hbm, cv_hbm, beam_ref, par_ref, dg_ref, dec_hbm,
     enc_hbm, ctx_ref,
-    tok, xl, xr, wbuf, wo, acc, qkv, att, attp, enc, decw,
+    tok, xl, xr, wbuf, wo, acc, qkv, att, attp, decw,
     sq, sqp, inv, gq, sc, scp, mix, mixp, bd, dn, dnr, dqp, dqr, stat, stats, ctf, ctp, cts, xs, ckb, gpart, gqa, gqp,
     lsem, tsend, trecv, psend, precv, ssend, srecv, csend, crecv, gsend, grecv,
 ):
     npsg, npb = sizes
+    enc = xl
     rows, half = tok.shape
     width = 2 * half
     cols = qkv.shape[2]
@@ -162,11 +163,12 @@
         copy_w[w][0].wait()
 
         def first_half(j, c):
-            t = pl.ds(pl.multiple_of(j * nt, nt), nt)
+            t = slice(j * nt, j * nt + nt)
             acc[w, :, t] = nn_dot(xl[...], wbuf[w, 0, :, t])
             return c
 
-        lax.fori_loop(0, cols // nt, first_half, 0)
+        for j in range(cols // nt):
+            first_half(j, 0)
         if w == 1:
             for s in send_dn:
                 s.wait()
@@ -197,12 +199,13 @@
         copy_w[w][1].wait()
 
         def second_half(j, c):
-            t = pl.ds(pl.multiple_of(j * nt, nt), nt)
+            t = slice(j * nt, j * nt + nt)
             scale = jnp.concatenate([inv[...]] * (nt // 128), axis=1)
             qkv[w, :, t] = ((acc[w, :, t] + nn_dot(xr[...], wbuf[w, 1, :, t])) * scale).astype(BF16)
             return c
 
-        lax.fori_loop(0, cols // nt, second_half, 0)
+        for j in range(cols // nt):
+            second_half(j, 0)
         if w == 0:
             copy_cv[0].start()
             copy_cv[1].start()
@@ -268,12 +271,13 @@
     copy_wo.wait()
 
     def out_own(j, c):
-        t = pl.ds(pl.multiple_of(j * nt, nt), nt)
+        t = slice(j * nt, j * nt + nt)
         per = cols // nt
-        acc[j // per, :, pl.ds(pl.multiple_of((j % per) * nt, nt), nt)] = nn_dot(att[...], wo[0, :, t])
-        return c
-
-    lax.fori_loop(0, half // nt, out_own, 0)
+        acc[j // per, :, slice((j % per) * nt, (j % per) * nt + nt)] = nn_dot(att[...], wo[0, :, t])
+        return c
+
+    for j in range(half // nt):
+        out_own(j, 0)
     for s in send_att:
         s.wait()
     send_gq.wait()
@@ -284,9 +288,9 @@
     sc[0 : 2 * hb, :] = jnp.zeros((2 * hb, rows), F32)
 
     def out_peer(j, c):
-        t = pl.ds(pl.multiple_of(j * nt, nt), nt)
+        t = slice(j * nt, j * nt + nt)
         per = cols // nt
-        a = acc[j // per, :, pl.ds(pl.multiple_of((j % per) * nt, nt), nt)]
+        a = acc[j // per, :, slice((j % per) * nt, (j % per) * nt + nt)]
         e = (tok[:, t].astype(F32) + (a + nn_dot(attp[...], wo[1, :, t]))).astype(BF16)
         enc[:, t] = e
         wide = e.astype(F32)
@@ -294,7 +298,8 @@
         sc[0 : 2 * hb, :] += nt_dot(gq[:, t], e)
         return c
 
-    lax.fori_loop(0, half // nt, out_peer, 0)
+    for j in range(half // nt):
+        out_peer(j, 0)
     copy_enc = pltpu.make_async_copy(enc, enc_hbm, lsem.at[13])
     sc[2 * hb : 2 * hb + 8, :] = jnp.broadcast_to(jnp.sum(jnp.transpose(sq[...]), axis=0, keepdims=True), (8, rows))
     send_sc = to_other(sc, scp, 4 + groups)
@@ -395,16 +400,17 @@
     copy_enc.wait()
 
 
-def writer(enc_hbm, ctx_in, enc_out, ctx_out, held, sem_in, sem_out):
-    n = sem_in.shape[0]
+def writer(enc_hbm, ctx_hbm, enc_out, ctx_out, held, ctx, sem_in, sem_out):
+    n = sem_in.shape[0] - 1
     rows = enc_hbm.shape[0] // n
     part = [pl.ds(i * rows, rows) for i in range(n)]
     ins = [pltpu.make_async_copy(enc_hbm.at[p, :], held.at[p, :], sem_in.at[i]) for i, p in enumerate(part)]
+    ins.append(pltpu.make_async_copy(ctx_hbm, ctx, sem_in.at[n]))
     outs = [pltpu.make_async_copy(held.at[p, :], enc_out.at[p, :], sem_out.at[i]) for i, p in enumerate(part)]
+    outs.append(pltpu.make_async_copy(ctx, ctx_out, sem_out.at[n]))
     for c in ins:
         c.start()
-    ctx_out[...] = ctx_in[...]
-    for i in range(n):
+    for i in range(n + 1):
         ins[i].wait()
         outs[i].start()
     for c in outs:
@@ -446,7 +452,6 @@
             V((3, rows, cols), BF16),
             V((rows, cols), BF16),
             V((rows, cols), BF16),
-            V((rows, half), BF16),
             V((width // npb, cols), BF16),
             V((rows, 128), F32),
             V((rows, 128), F32),
@@ -497,9 +502,9 @@
             jax.ShapeDtypeStruct((rows, half), BF16),
             jax.ShapeDtypeStruct((beams, cols), F32),
         ),
-        in_specs=[hbm, vmem],
-        out_specs=(hbm, vmem),
-        scratch_shapes=[V((rows, half), BF16), D((8,)), D((8,))],
+        in_specs=[hbm, hbm],
+        out_specs=(hbm, hbm),
+        scratch_shapes=[V((rows, half), BF16), V((beams, cols), F32), D((9,)), D((9,))],
     )(encoded, context)
     return (
         encoded.reshape(questions, passages, plen, half),

time: 53 us -> 49.1 us (0.926)
  Pallas kernels: 52 us -> 48.1 us
    pallas_call x1, Pallas kernels: 48.3 us -> 45.7 us  [per_device(): pl.pallas_call(functools.partial(body, (npsg, npb)), out_shape=(jax.Shape...]
    pallas_call x1, Pallas kernels: 3.72 us -> 2.41 us  [per_device(): pl.pallas_call(writer, out_shape=(jax.ShapeDtypeStruct((rows, half), BF16...]
where the time goes in v5:
time: 49.1 us; the launch traced here: 48.9 us
  Pallas kernels  48.1 us (98%)
  between operations  0.8 us (2%)
    pallas_call x1, Pallas kernels, per_device(): pl.pallas_call(functools.partial(body, (npsg, npb)), out_shape=(jax.Shape...  45.7 us
    pallas_call x1, Pallas kernels, per_device(): pl.pallas_call(writer, out_shape=(jax.ShapeDtypeStruct((rows, half), BF16...  2.41 us

profile of v5, /device:TPU:0, one launch (start us, length us, event | category | flops | bytes accessed | tf_op | source)
XLA Modules:
  0.0 48.9 jit_solution(15812406805080627668)
XLA Ops:
  0.6 45.7 %shard_map.149 = (bf16[512,2048]{1,0:T(8,128)(2,1)}, f32[4,1024]{1,0:T(4,128)}) custom-call(bf16[512,2048]{1,0:T(8,128)(2,1)} %bitcast.7, s32[1,32]{1,0:T(1,128)} %len_ref.1, f32[1,4096]{1,0:T(1,128)} %bitcast.9, bf16[4096,1024]{1,0:T(8,128)(2,1)} %wq_hbm.1, bf16[4096,1024]{1,0:T(8,128)(2,1)} %wk_hbm.1, bf16[4096,1024]{1,0:T(8,128)(2,1)} %wv_hbm.1, ...), custom_call_target="tpu_custom_call" | custom-call | tf_op jit(solution)/shard_map/pallas_call | solution.py:437
  46.3 2.4 %shard_map.150 = (bf16[512,2048]{1,0:T(8,128)(2,1)}, f32[4,1024]{1,0:T(4,128)}) custom-call(bf16[512,2048]{1,0:T(8,128)(2,1)} %get-tuple-element.6.enc_hbm, f32[4,1024]{1,0:T(4,128)} %get-tuple-element.7.ctx_hbm), custom_call_target="tpu_custom_call" | custom-call | tf_op jit(solution)/shard_map/pallas_call | solution.py:499

commit v6 on v5

--- a/solution.py
+++ b/solution.py
@@ -1,4 +1,5 @@
 import functools
+import math
 
 import jax
 import jax.numpy as jnp
@@ -34,11 +35,11 @@
 
 def body(
     sizes,
-    tok_hbm, len_ref, eg_ref, wq_hbm, wk_hbm, wv_hbm, wo_hbm, fg_ref, ck_hbm, cv_hbm, beam_ref, par_ref, dg_ref, dec_hbm,
+    tok_hbm, len_hbm, eg_hbm, wq_hbm, wk_hbm, wv_hbm, wo_hbm, fg_hbm, ck_hbm, cv_hbm, beam_hbm, par_hbm, dg_hbm, dec_hbm,
     enc_hbm, ctx_ref,
     tok, xl, xr, wbuf, wo, acc, qkv, att, attp, decw,
-    sq, sqp, inv, gq, sc, scp, mix, mixp, bd, dn, dnr, dqp, dqr, stat, stats, ctf, ctp, cts, xs, ckb, gpart, gqa, gqp,
-    lsem, tsend, trecv, psend, precv, ssend, srecv, csend, crecv, gsend, grecv,
+    sq, sqp, inv, gq, sc, scp, mix, mixp, bd, dn, dnr, dqp, dqr, stat, stats, ctf, ctp, cts, xs, ckb, gpart, gqa, gqp, len_ref, par_ref, eg_ref, fg_ref, dg_ref, beam_ref,
+    lsem, tsend, trecv, psend, precv, ssend, srecv, csend, crecv, gsend, grecv, msem,
 ):
     npsg, npb = sizes
     enc = xl
@@ -57,17 +58,10 @@
     mine_f = pl.ds(pl.multiple_of(tp * half, half), half)
     peer_f = pl.ds(pl.multiple_of(other * half, half), half)
 
-    barrier = pltpu.get_barrier_semaphore()
-    pl.semaphore_signal(barrier, inc=1, device_id={"tp": other}, device_id_type=MESH)
-
-    def hello_psg(k, c):
-        pl.semaphore_signal(barrier, inc=1, device_id={"psg": lax.rem(psg + k, npsg)}, device_id_type=MESH)
-        return c
-
-    lax.fori_loop(1, npsg, hello_psg, 0)
-    for k in range(1, npb):
-        pl.semaphore_signal(barrier, inc=1, device_id={"pb": lax.rem(pb + k, npb)}, device_id_type=MESH)
-
+    small = (beam_hbm, beam_ref), (par_hbm, par_ref), (dg_hbm, dg_ref), (eg_hbm, eg_ref), (fg_hbm, fg_ref), (len_hbm, len_ref)
+    small = [pltpu.make_async_copy(a, b, msem.at[i]) for i, (a, b) in enumerate(small)]
+    for c in small:
+        c.start()
     parts = 4
     prow = rows // parts
     copy_tok = [
@@ -76,6 +70,17 @@
     ]
     for c in copy_tok:
         c.start()
+    barrier = pltpu.get_barrier_semaphore()
+    pl.semaphore_signal(barrier, inc=1, device_id={"tp": other}, device_id_type=MESH)
+
+    def hello_psg(k, c):
+        pl.semaphore_signal(barrier, inc=1, device_id={"psg": lax.rem(psg + k, npsg)}, device_id_type=MESH)
+        return c
+
+    lax.fori_loop(1, npsg, hello_psg, 0)
+    for k in range(1, npb):
+        pl.semaphore_signal(barrier, inc=1, device_id={"pb": lax.rem(pb + k, npb)}, device_id_type=MESH)
+
     w_hbm = (wq_hbm, wk_hbm, wv_hbm)
     copy_w = [[None, None] for _ in range(3)]
     for h, part in enumerate((mine_f, peer_f)):
@@ -97,6 +102,8 @@
         copy_w[w][1].start()
     copy_wo.start()
 
+    for c in small:
+        c.wait()
     chosen = []
     for b in range(beams):
         row = jnp.zeros((1, width), F32)
@@ -147,10 +154,16 @@
             device_id={"pb": to}, device_id_type=MESH,
         )
 
+    side = math.isqrt(npsg)
+    away = sorted(range(1, npsg), key=lambda k: -sum(min(c, side - c) for c in divmod(k, side)))
+
+    def psg_at(k):
+        return lax.rem(psg // side + k // side, side) * side + lax.rem(psg % side + k % side, side)
+
     def to_psg(k, src, dst, ss, rs):
         return pltpu.make_async_remote_copy(
             src_ref=src, dst_ref=dst, send_sem=ss.at[k - 1], recv_sem=rs.at[k - 1],
-            device_id={"psg": lax.rem(psg + k, npsg)}, device_id_type=MESH,
+            device_id={"psg": psg_at(k)}, device_id_type=MESH,
         )
 
     send_dn = [to_pb(k, dn, dnr, 0) for k in range(1, npb)]
@@ -224,11 +237,8 @@
                 gain = fg_ref[:, pl.ds(pl.multiple_of(c * half + psg * fc, fc), fc)]
                 gpart[f] = (nt_dot(bd[...], ckb[f]) * gain).astype(BF16)
 
-            def start_gq(k, c):
+            for k in away:
                 to_psg(k, gpart, gqa.at[:, psg], gsend, grecv).start()
-                return c
-
-            lax.fori_loop(1, npsg, start_gq, 0)
             gqa[:, psg] = gpart[...]
 
     lane = lax.broadcasted_iota(jnp.int32, (plen, 128), 1)
@@ -255,19 +265,6 @@
         s.start()
         send_att.append(s)
 
-    mine_h = pl.ds(pl.multiple_of(tp * hb, hb), hb)
-    peer_h = pl.ds(pl.multiple_of(other * hb, hb), hb)
-
-    def wait_gq(k, c):
-        to_psg(k, gpart, gqa.at[:, psg], gsend, grecv).wait()
-        return c
-
-    lax.fori_loop(1, npsg, wait_gq, 0)
-    send_gq = to_other(gqa.at[1], gqp, 3 + groups)
-    send_gq.start()
-    for i in range(npsg):
-        gq[mine_h, i * fc : (i + 1) * fc] = gqa[0, i]
-
     copy_wo.wait()
 
     def out_own(j, c):
@@ -278,14 +275,20 @@
 
     for j in range(half // nt):
         out_own(j, 0)
+    mine_h = pl.ds(pl.multiple_of(tp * hb, hb), hb)
+    peer_h = pl.ds(pl.multiple_of(other * hb, hb), hb)
+
+    for k in away:
+        to_psg(k, gpart, gqa.at[:, psg], gsend, grecv).wait()
+    send_gq = to_other(gqa.at[1], gqp, 3 + groups)
+    send_gq.start()
+    for i in range(npsg):
+        gq[mine_h, i * fc : (i + 1) * fc] = gqa[0, i]
+
     for s in send_att:
         s.wait()
-    send_gq.wait()
-    for i in range(npsg):
-        gq[peer_h, i * fc : (i + 1) * fc] = gqp[i]
     send_wo.wait()
     sq[...] = jnp.zeros_like(sq)
-    sc[0 : 2 * hb, :] = jnp.zeros((2 * hb, rows), F32)
 
     def out_peer(j, c):
         t = slice(j * nt, j * nt + nt)
@@ -295,11 +298,14 @@
         enc[:, t] = e
         wide = e.astype(F32)
         sq[...] += lane_fold(wide * wide)
-        sc[0 : 2 * hb, :] += nt_dot(gq[:, t], e)
         return c
 
     for j in range(half // nt):
         out_peer(j, 0)
+    send_gq.wait()
+    for i in range(npsg):
+        gq[peer_h, i * fc : (i + 1) * fc] = gqp[i]
+    sc[0 : 2 * hb, :] = nt_dot(gq[...], enc[...])
     copy_enc = pltpu.make_async_copy(enc, enc_hbm, lsem.at[13])
     sc[2 * hb : 2 * hb + 8, :] = jnp.broadcast_to(jnp.sum(jnp.transpose(sq[...]), axis=0, keepdims=True), (8, rows))
     send_sc = to_other(sc, scp, 4 + groups)
@@ -321,23 +327,17 @@
     wt = (e * iv).astype(BF16)
     total = jnp.sum(wt.astype(F32) * (x * iv), axis=1, keepdims=True)
 
-    def mixed(j, c):
-        t = pl.ds(pl.multiple_of(j * nt, nt), nt)
+    for j in range(half // nt):
+        t = slice(j * nt, j * nt + nt)
         gain = fg_ref[:, pl.ds(pl.multiple_of(tp * half + j * nt, nt), nt)]
         mix[:, t] = (nn_dot(wt, enc[:, t]) * gain).astype(BF16)
-        return c
-
-    lax.fori_loop(0, half // nt, mixed, 0)
     send_mix = to_other(mix.at[peer_h, :], mixp, 5 + groups)
     send_mix.start()
     first = lax.broadcasted_iota(jnp.int32, (2 * hb, 128), 1) == 0
     stat[...] = jnp.transpose(jnp.where(first, peak, total))[0:8, :]
 
-    def start_stat(k, c):
+    for k in away:
         to_psg(k, stat, stats.at[psg], ssend, srecv).start()
-        return c
-
-    lax.fori_loop(1, npsg, start_stat, 0)
     stats[psg] = stat[...]
 
 
@@ -360,18 +360,12 @@
             ctf[r : r + 1, :] = jnp.sum(m[b * heads : (b + 1) * heads], axis=0, keepdims=True)
     ctp[...] = ctf[...].astype(BF16)
 
-    def start_ctx(k, c):
+    for k in away:
         to_psg(k, ctp, cts.at[psg], csend, crecv).start()
-        return c
-
-    lax.fori_loop(1, npsg, start_ctx, 0)
     cts[psg] = ctp[...]
 
-    def wait_stat(k, c):
+    for k in away:
         to_psg(k, stat, stats.at[psg], ssend, srecv).wait()
-        return c
-
-    lax.fori_loop(1, npsg, wait_stat, 0)
     peaks = stats[:, 0:1, :]
     factor = jnp.exp2((peaks - jnp.max(peaks, axis=0, keepdims=True)) * LOG2E)
     factor = factor / jnp.sum(stats[:, 1:2, :] * factor, axis=0, keepdims=True)
@@ -389,11 +383,8 @@
     one = jnp.where(one, 1.0, 0.0).astype(BF16)
     xs[...] = (nn_dot(coarse, one) + nn_dot(fine, one)).reshape(npsg, nr, ct)
 
-    def wait_ctx(k, c):
+    for k in away:
         to_psg(k, ctp, cts.at[psg], csend, crecv).wait()
-        return c
-
-    lax.fori_loop(1, npsg, wait_ctx, 0)
     whole = jnp.sum(cts[...].astype(F32) * xs[...], axis=0)
     for g in range(cols // ct):
         ctx_ref[:, g * ct : (g + 1) * ct] = whole[g * beams : (g + 1) * beams, :]
@@ -431,7 +422,6 @@
     npsg, npb = lax.axis_size("psg"), lax.axis_size("pb")
     groups = cols // 256
     vmem = pl.BlockSpec(memory_space=pltpu.VMEM)
-    smem = pl.BlockSpec(memory_space=pltpu.SMEM)
     hbm = pl.BlockSpec(memory_space=pl.ANY)
     V, D = pltpu.VMEM, pltpu.SemaphoreType.DMA
     encoded, context = pl.pallas_call(
@@ -440,7 +430,7 @@
             jax.ShapeDtypeStruct((rows, half), BF16),
             jax.ShapeDtypeStruct((beams, cols), F32),
         ),
-        in_specs=[hbm, smem, vmem, hbm, hbm, hbm, hbm, vmem, hbm, hbm, vmem, smem, vmem, hbm],
+        in_specs=[hbm] * 14,
         out_specs=(hbm, vmem),
         scratch_shapes=[
             V((rows, half), BF16),
@@ -476,6 +466,12 @@
             V((2, hb, half // npsg), BF16),
             V((2, npsg, hb, half // npsg), BF16),
             V((npsg, hb, half // npsg), BF16),
+            pltpu.SMEM(lengths.shape, jnp.int32),
+            pltpu.SMEM(parents.shape, jnp.int32),
+            V((1, width), F32),
+            V((1, width), F32),
+            V((1, width), F32),
+            V((beams, width), BF16),
             D((16,)),
             D((6 + groups,)),
             D((6 + groups,)),
@@ -487,6 +483,7 @@
             D((npsg - 1,)),
             D((npsg - 1,)),
             D((npsg - 1,)),
+            D((6,)),
         ],
         compiler_params=pltpu.CompilerParams(
             collective_id=0, has_side_effects=True, vmem_limit_bytes=60 * 2**20

time: 49.1 us -> 47.3 us (0.963)
  Pallas kernels: 48.1 us -> 46.2 us
    pallas_call x1, Pallas kernels: 45.7 us -> 43.8 us  [per_device(): pl.pallas_call(functools.partial(body, (npsg, npb)), out_shape=(jax.Shape...]
where the time goes in v6:
time: 47.3 us; the launch traced here: 47 us
  Pallas kernels  46.2 us (98%)
  between operations  0.8 us (2%)
    pallas_call x1, Pallas kernels, per_device(): pl.pallas_call(functools.partial(body, (npsg, npb)), out_shape=(jax.Shape...  43.8 us
    pallas_call x1, Pallas kernels, per_device(): pl.pallas_call(writer, out_shape=(jax.ShapeDtypeStruct((rows, half), BF16...  2.41 us

profile of v6, /device:TPU:0, one launch (start us, length us, event | category | flops | bytes accessed | tf_op | source)
XLA Modules:
  0.0 47.0 jit_solution(13311196675585613971)
XLA Ops:
  0.6 43.8 %shard_map.149 = (bf16[512,2048]{1,0:T(8,128)(2,1)}, f32[4,1024]{1,0:T(4,128)}) custom-call(bf16[512,2048]{1,0:T(8,128)(2,1)} %bitcast.7, s32[1,32]{1,0:T(1,128)} %len_hbm.1, f32[1,4096]{1,0:T(1,128)} %bitcast.9, bf16[4096,1024]{1,0:T(8,128)(2,1)} %wq_hbm.1, bf16[4096,1024]{1,0:T(8,128)(2,1)} %wk_hbm.1, bf16[4096,1024]{1,0:T(8,128)(2,1)} %wv_hbm.1, ...), custom_call_target="tpu_custom_call" | custom-call | tf_op jit(solution)/shard_map/pallas_call | solution.py:427
  44.4 2.4 %shard_map.150 = (bf16[512,2048]{1,0:T(8,128)(2,1)}, f32[4,1024]{1,0:T(4,128)}) custom-call(bf16[512,2048]{1,0:T(8,128)(2,1)} %get-tuple-element.6.enc_hbm, f32[4,1024]{1,0:T(4,128)} %get-tuple-element.7.ctx_hbm), custom_call_target="tpu_custom_call" | custom-call | tf_op jit(solution)/shard_map/pallas_call | solution.py:496

commit v7 on v6

--- a/solution.py
+++ b/solution.py
@@ -246,24 +246,39 @@
     slot = lax.broadcasted_iota(jnp.int32, (1, plen), 1)
     groups = cols // 256
     send_att = []
-    for g in range(groups):
-        for p in range(passages):
-            key_live = slot < len_ref[0, psg * passages + p]
-            r = slice(p * plen, (p + 1) * plen)
-            for pair in range(2):
-                t = slice(g * 256 + pair * 128, g * 256 + pair * 128 + 128)
-                q = qkv[0, r, t]
-                zero = jnp.zeros_like(q)
-                q2 = jnp.concatenate([jnp.where(low, q, zero), jnp.where(low, zero, q)], axis=0)
-                s = jnp.where(key_live, nt_dot(q2, qkv[1, r, t]), NEGATIVE)
-                e = jnp.exp2((s - jnp.max(s, axis=-1, keepdims=True)) * (SCALE * LOG2E))
-                den = jnp.sum(e, axis=-1, keepdims=True)
-                o = nn_dot(e.astype(BF16), qkv[2, r, t]) / den
-                att[r, t] = jnp.where(low, o[:plen], o[plen:]).astype(BF16)
-        t = slice(g * 256, g * 256 + 256)
-        s = to_other(att.at[:, t], attp.at[:, t], 3 + g)
-        s.start()
-        send_att.append(s)
+
+    def logits(p, t):
+        r = slice(p * plen, (p + 1) * plen)
+        q = qkv[0, r, t]
+        zero = jnp.zeros_like(q)
+        q2 = jnp.concatenate([jnp.where(low, q, zero), jnp.where(low, zero, q)], axis=0)
+        return nt_dot(q2, qkv[1, r, t])
+
+    units = [(p, slice(h * 128, h * 128 + 128)) for g in range(groups) for p in range(passages) for h in (2 * g, 2 * g + 1)]
+    following = logits(*units[0])
+
+    def blend(i, e, den):
+        p, t = units[i]
+        r = slice(p * plen, (p + 1) * plen)
+        o = nn_dot(e, qkv[2, r, t]) * den
+        att[r, t] = jnp.where(low, o[:plen], o[plen:]).astype(BF16)
+        if i % (2 * passages) == 2 * passages - 1:
+            g = i // (2 * passages)
+            t = slice(g * 256, g * 256 + 256)
+            send = to_other(att.at[:, t], attp.at[:, t], 3 + g)
+            send.start()
+            send_att.append(send)
+
+    before = None
+    for i, (p, t) in enumerate(units):
+        s = jnp.where(slot < len_ref[0, psg * passages + p], following, NEGATIVE)
+        if i + 1 < len(units):
+            following = logits(*units[i + 1])
+        if before is not None:
+            blend(i - 1, *before)
+        e = jnp.exp2((s - jnp.max(s, axis=-1, keepdims=True)) * (SCALE * LOG2E))
+        before = e.astype(BF16), 1.0 / jnp.sum(e, axis=-1, keepdims=True)
+    blend(len(units) - 1, *before)
 
     copy_wo.wait()
 

time: 47.3 us -> 47 us (level)
  no operation moved by 1% of the time
where the time goes in v7:
time: 47 us; the launch traced here: 46.7 us
  Pallas kernels  45.9 us (98%)
  between operations  0.8 us (2%)
    pallas_call x1, Pallas kernels, per_device(): pl.pallas_call(functools.partial(body, (npsg, npb)), out_shape=(jax.Shape...  43.5 us
    pallas_call x1, Pallas kernels, per_device(): pl.pallas_call(writer, out_shape=(jax.ShapeDtypeStruct((rows, half), BF16...  2.41 us

profile of v7, /device:TPU:0, one launch (start us, length us, event | category | flops | bytes accessed | tf_op | source)
XLA Modules:
  0.0 46.7 jit_solution(6942298974524009245)
XLA Ops:
  0.6 43.5 %shard_map.149 = (bf16[512,2048]{1,0:T(8,128)(2,1)}, f32[4,1024]{1,0:T(4,128)}) custom-call(bf16[512,2048]{1,0:T(8,128)(2,1)} %bitcast.7, s32[1,32]{1,0:T(1,128)} %len_hbm.1, f32[1,4096]{1,0:T(1,128)} %bitcast.9, bf16[4096,1024]{1,0:T(8,128)(2,1)} %wq_hbm.1, bf16[4096,1024]{1,0:T(8,128)(2,1)} %wk_hbm.1, bf16[4096,1024]{1,0:T(8,128)(2,1)} %wv_hbm.1, ...), custom_call_target="tpu_custom_call" | custom-call | tf_op jit(solution)/shard_map/pallas_call | solution.py:442
  44.1 2.4 %shard_map.150 = (bf16[512,2048]{1,0:T(8,128)(2,1)}, f32[4,1024]{1,0:T(4,128)}) custom-call(bf16[512,2048]{1,0:T(8,128)(2,1)} %get-tuple-element.6.enc_hbm, f32[4,1024]{1,0:T(4,128)} %get-tuple-element.7.ctx_hbm), custom_call_target="tpu_custom_call" | custom-call | tf_op jit(solution)/shard_map/pallas_call | solution.py:511

commit v8 on v7

--- a/solution.py
+++ b/solution.py
@@ -257,11 +257,15 @@
     units = [(p, slice(h * 128, h * 128 + 128)) for g in range(groups) for p in range(passages) for h in (2 * g, 2 * g + 1)]
     following = logits(*units[0])
 
-    def blend(i, e, den):
+    def blend(i, e):
         p, t = units[i]
         r = slice(p * plen, (p + 1) * plen)
-        o = nn_dot(e, qkv[2, r, t]) * den
-        att[r, t] = jnp.where(low, o[:plen], o[plen:]).astype(BF16)
+        v = qkv[2, r, t]
+        one = jnp.ones_like(v)
+        o0 = nn_dot(e[:plen], jnp.where(low, v, one))
+        o1 = nn_dot(e[plen:], jnp.where(low, one, v))
+        den = pltpu.roll(jnp.where(low, o1, o0), DH, 1)
+        att[r, t] = (jnp.where(low, o0, o1) / den).astype(BF16)
         if i % (2 * passages) == 2 * passages - 1:
             g = i // (2 * passages)
             t = slice(g * 256, g * 256 + 256)
@@ -275,10 +279,10 @@
         if i + 1 < len(units):
             following = logits(*units[i + 1])
         if before is not None:
-            blend(i - 1, *before)
+            blend(i - 1, before)
         e = jnp.exp2((s - jnp.max(s, axis=-1, keepdims=True)) * (SCALE * LOG2E))
-        before = e.astype(BF16), 1.0 / jnp.sum(e, axis=-1, keepdims=True)
-    blend(len(units) - 1, *before)
+        before = e.astype(BF16)
+    blend(len(units) - 1, before)
 
     copy_wo.wait()
 

time: 47 us -> 47.1 us (level)
  no operation moved by 1% of the time
where the time goes in v8:
time: 47.1 us; the launch traced here: 46.8 us
  Pallas kernels  46 us (98%)
  between operations  0.8 us (2%)
    pallas_call x1, Pallas kernels, per_device(): pl.pallas_call(functools.partial(body, (npsg, npb)), out_shape=(jax.Shape...  43.6 us
    pallas_call x1, Pallas kernels, per_device(): pl.pallas_call(writer, out_shape=(jax.ShapeDtypeStruct((rows, half), BF16...  2.41 us

profile of v8, /device:TPU:0, one launch (start us, length us, event | category | flops | bytes accessed | tf_op | source)
XLA Modules:
  0.0 46.8 jit_solution(6115105603573607864)
XLA Ops:
  0.6 43.6 %shard_map.149 = (bf16[512,2048]{1,0:T(8,128)(2,1)}, f32[4,1024]{1,0:T(4,128)}) custom-call(bf16[512,2048]{1,0:T(8,128)(2,1)} %bitcast.7, s32[1,32]{1,0:T(1,128)} %len_hbm.1, f32[1,4096]{1,0:T(1,128)} %bitcast.9, bf16[4096,1024]{1,0:T(8,128)(2,1)} %wq_hbm.1, bf16[4096,1024]{1,0:T(8,128)(2,1)} %wk_hbm.1, bf16[4096,1024]{1,0:T(8,128)(2,1)} %wv_hbm.1, ...), custom_call_target="tpu_custom_call" | custom-call | tf_op jit(solution)/shard_map/pallas_call | solution.py:446
  44.2 2.4 %shard_map.150 = (bf16[512,2048]{1,0:T(8,128)(2,1)}, f32[4,1024]{1,0:T(4,128)}) custom-call(bf16[512,2048]{1,0:T(8,128)(2,1)} %get-tuple-element.6.enc_hbm, f32[4,1024]{1,0:T(4,128)} %get-tuple-element.7.ctx_hbm), custom_call_target="tpu_custom_call" | custom-call | tf_op jit(solution)/shard_map/pallas_call | solution.py:515
